TPU v7x, 512 devices: a whole 4x4x16 slice. The times are simulated.
512 devices in a mesh: gx: 64 (over x_lo, z, core), gz: 8 (over y, x_hi).
Axes of the slice: x: 4 (x_hi: 2, x_lo: 2; x = x_hi * 2 + x_lo), y: 4, z: 16, core: 2. Of those that a mesh axis runs over, the one named last changes fastest.
Arguments:
- particle_drag: bfloat16 [64, 8, 4, 2048], P('gx', 'gz'), may hold values from -48 to 48
- particle_weights: bfloat16 [64, 8, 2048, 128], P('gx', 'gz'), may hold values from 0 to 1
- migration_counts: int32 [64, 8, 5], P('gx', 'gz'), may hold values from 0 to 1792, as said below
- tile_owner: int32 [64, 8, 384, 1], P('gx', 'gz'), may hold values from 0 to 8; in each aligned block of 384 rows (0 to 383, 384 to 767, ..., all dimensions but the last counted through in order) at most 128 rows name the same one
- tile_column: int32 [64, 8, 384], P('gx', 'gz'), may hold values from 0 to 1023
Outputs:
- filtered_source: float32 [2048, 256, 4, 128], P('gx', 'gz')
Inputs may be any that keep to these rules, and one draw needn't show every extreme that they name: migration_counts[a, b, 0] is 2048 minus the other four; each of migration_counts[a, b, 1..4] is at most 256, and on every device one of them equals 256; on some device the other three are 0, so that it keeps 2048 - 256. `tile_owner`: on each device at most 128 tiles carry the same code, and on some device some code is carried by exactly 128 tiles.
All inputs are finite; a program needn't handle non-finite values.
Results may differ from a plain program's by a relative error of at most 0.00035.
Values may be sent and summed in bfloat16 or wider, within the bound.
A program may use at most 64 MiB of HBM per device.

v0:
```python
import math

import jax
import jax.numpy as jnp
from jax import lax
from jax.sharding import PartitionSpec as P

CX = 32
CZ = 32
NY = 128
P_SIZE = 2048
G = 8
REACH = 4
M = 256
KT = 128


def for_sending(shard):
    return jax.tree.map(lambda a: a.astype(jnp.bfloat16) if a.dtype == jnp.float32 else a, shard)


def passed_along(value, axis, steps):
    count = lax.axis_size(axis)
    pairs = [(source, (source + steps) % count) for source in range(count)]
    return lax.ppermute(value, axis, pairs)


def padded(block, sides, width):
    for axis, dim in sides:
        count = lax.axis_size(axis)
        forward = [(i, i + 1) for i in range(count - 1)]
        forward.append((count - 1, 0))
        backward = [(target, source) for source, target in forward]
        low = lax.ppermute(
            lax.slice_in_dim(block, block.shape[dim] - width, None, axis=dim), axis, forward
        )
        high = lax.ppermute(lax.slice_in_dim(block, 0, width, axis=dim), axis, backward)
        block = jnp.concatenate([low, block, high], axis=dim)
    return block


def gauss_taps():
    raw_values = [
        math.exp(-offset_value * offset_value / 8.0) for offset_value in range(-REACH, REACH + 1)
    ]
    total_value = sum(raw_values)
    return [raw_entry / total_value for raw_entry in raw_values]


def deposit_tiles(part_drag, part_weights):
    channel_count = part_drag.shape[0]
    groups_count = part_drag.shape[1] // G
    drag_groups = part_drag.reshape(channel_count, groups_count, G)
    weight_groups = part_weights.reshape(groups_count, G, NY)
    tiles_made = jnp.einsum(
        "ctg,tgy->tcy", drag_groups, weight_groups, preferred_element_type=jnp.float32
    )
    return tiles_made.reshape(groups_count, channel_count * NY)


def local(particle_drag, particle_weights, migration_counts, tile_owner, tile_column):
    local_drag = particle_drag[0, 0]
    local_weights = particle_weights[0, 0]
    count_row = migration_counts[0, 0]
    dest_codes = tile_owner[0, 0, :, 0]
    column_ids = tile_column[0, 0]
    channel_count = local_drag.shape[0]
    width_flat = channel_count * NY
    starts_at = jnp.cumsum(count_row) - count_row
    slot_ids = jnp.arange(P_SIZE)
    kept_drag = jnp.where(slot_ids[None, :] < count_row[0], local_drag, jnp.zeros_like(local_drag))
    padded_drag = jnp.concatenate(
        [local_drag, jnp.zeros((channel_count, M), local_drag.dtype)], axis=1
    )
    padded_weights = jnp.concatenate(
        [local_weights, jnp.zeros((M, NY), local_weights.dtype)], axis=0
    )
    lane_ids = jnp.arange(M)

    def outgoing(direction):
        start_slot = starts_at[direction]
        sent_drag = lax.dynamic_slice_in_dim(padded_drag, start_slot, M, 1)
        sent_drag = jnp.where(
            lane_ids[None, :] < count_row[direction], sent_drag, jnp.zeros_like(sent_drag)
        )
        sent_weights = lax.dynamic_slice_in_dim(padded_weights, start_slot, M, 0)
        return (sent_drag, sent_weights)

    tile_parts = [deposit_tiles(kept_drag, local_weights)]
    for direction, shift_by in ((1, 1), (2, -1)):
        arrived = passed_along(for_sending(outgoing(direction)), "gx", shift_by)
        tile_parts.append(deposit_tiles(arrived[0], arrived[1]))
    for direction, shift_by in ((3, 1), (4, -1)):
        arrived = passed_along(for_sending(outgoing(direction)), "gz", shift_by)
        tile_parts.append(deposit_tiles(arrived[0], arrived[1]))
    all_tiles = jnp.concatenate(tile_parts, axis=0)
    code_hits = (dest_codes[:, None] == jnp.arange(9)[None, :]).astype(jnp.int32)
    code_ranks = jnp.sum((jnp.cumsum(code_hits, axis=0) - code_hits) * code_hits, axis=1)
    slot_of = dest_codes * KT + code_ranks
    placer = (slot_of[:, None] == jnp.arange(9 * KT)[None, :]).astype(jnp.float32)
    buckets = jnp.einsum("ts,tf->sf", placer, all_tiles, precision=lax.Precision.HIGHEST)
    spot_values = jnp.einsum(
        "ts,t->s", placer, column_ids.astype(jnp.float32), precision=lax.Precision.HIGHEST
    )
    buckets = buckets.reshape(3, 3, KT, width_flat)
    spot_values = spot_values.reshape(3, 3, KT)
    widened = (
        padded(buckets, (("gx", 0), ("gz", 1)), 1),
        padded(spot_values, (("gx", 0), ("gz", 1)), 1),
    )
    got_tiles = widened[0][::2, ::2].reshape(9 * KT, width_flat)
    got_spots = widened[1][::2, ::2].reshape(9 * KT)
    spot_ids = got_spots.astype(jnp.int32)
    column_hits = (spot_ids[:, None] == jnp.arange(CX * CZ)[None, :]).astype(jnp.float32)
    source_flat = jnp.einsum("sc,sf->cf", column_hits, got_tiles, precision=lax.Precision.HIGHEST)
    gauss_weights = gauss_taps()
    row_iota = lax.broadcasted_iota(jnp.int32, (NY, NY), 0)
    col_iota = lax.broadcasted_iota(jnp.int32, (NY, NY), 1)
    plane_gap = row_iota - col_iota
    band_matrix = jnp.zeros((NY, NY), jnp.float32)
    for tap_index in range(2 * REACH + 1):
        band_matrix = band_matrix + gauss_weights[tap_index] * (
            plane_gap == tap_index - REACH
        ).astype(jnp.float32)
    along_y = jnp.dot(
        source_flat.reshape(CX * CZ * channel_count, NY),
        band_matrix,
        precision=lax.Precision.HIGHEST,
    )
    along_y = along_y.reshape(CX, CZ, channel_count, NY)
    widened_x = padded(along_y, (("gx", 0),), REACH)
    along_x = gauss_weights[0] * widened_x[0:CX]
    for tap_index in range(1, 2 * REACH + 1):
        along_x = along_x + gauss_weights[tap_index] * widened_x[tap_index : tap_index + CX]
    widened_z = padded(along_x, (("gz", 1),), REACH)
    filtered = gauss_weights[0] * widened_z[:, 0:CZ]
    for tap_index in range(1, 2 * REACH + 1):
        filtered = filtered + gauss_weights[tap_index] * widened_z[:, tap_index : tap_index + CZ]
    return filtered


def solution(mesh):
    in_specs = (
        P("gx", "gz", None, None),
        P("gx", "gz", None, None),
        P("gx", "gz", None),
        P("gx", "gz", None, None),
        P("gx", "gz", None),
    )
    out_specs = P("gx", "gz", None, None)
    return jax.shard_map(local, mesh=mesh, in_specs=in_specs, out_specs=out_specs, check_vma=False)
```

profile of v0, /device:TPU:30, one launch (start us, length us, event | category | flops | bytes accessed | tf_op | source)
XLA Modules:
  0.0 190.7 jit_solution(3388572345667210734)
XLA Ops:
  17.8 3.9 %collective-permute-start.5 = (bf16[256,128]{1,0:T(8,128)(2,1)S(1)}, bf16[256,128]{1,0:T(8,128)(2,1)S(1)}, u32[]{:S(2)}, u32[]{:S(2)}) collective-permute-start(bf16[256,128]{1,0:T(8,128)(2,1)S(1)} %get-tuple-element.16), channel_id=1, source_target_pairs={{0,8},{8,16},{16,24},{24,32},{32,40},{40,48},{48,56},{56,64},{64,7... | collective-permute-start | bytes 196616 | tf_op jit(solution)/shard_map/ppermute | solution.py:25
  21.7 9.1 %collective-permute-start.6 = (bf16[4,256]{1,0:T(4,128)(2,1)S(1)}, bf16[4,256]{1,0:T(4,128)(2,1)S(1)}, u32[]{:S(2)}, u32[]{:S(2)}) collective-permute-start(bf16[4,256]{1,0:T(4,128)(2,1)S(1)} %get-tuple-element.18), channel_id=1, source_target_pairs={{0,504},{8,0},{16,8},{24,16},{32,24},{40,32},{48,40},{56,48},{64,5... | collective-permute-start | bytes 6152 | tf_op jit(solution)/shard_map/ppermute | solution.py:25
  30.9 2.6 %collective-permute-start.8 = (bf16[4,256]{1,0:T(4,128)(2,1)S(1)}, bf16[4,256]{1,0:T(4,128)(2,1)S(1)}, u32[]{:S(2)}, u32[]{:S(2)}) collective-permute-start(bf16[4,256]{1,0:T(4,128)(2,1)S(1)} %get-tuple-element.19), channel_id=1, source_target_pairs={{0,1},{1,2},{2,3},{3,4},{4,5},{5,6},{6,7},{7,0},{8,9},{9,10},{10,1... | collective-permute-start | bytes 6152 | tf_op jit(solution)/shard_map/ppermute | solution.py:25
  33.5 4.7 %collective-permute-start.10 = (bf16[4,256]{1,0:T(4,128)(2,1)S(1)}, bf16[4,256]{1,0:T(4,128)(2,1)S(1)}, u32[]{:S(2)}, u32[]{:S(2)}) collective-permute-start(bf16[4,256]{1,0:T(4,128)(2,1)S(1)} %get-tuple-element.17), channel_id=1, source_target_pairs={{0,7},{1,0},{2,1},{3,2},{4,3},{5,4},{6,5},{7,6},{8,15},{9,8},{10,9... | collective-permute-start | bytes 6152 | tf_op jit(solution)/shard_map/ppermute | solution.py:25
  43.8 4.9 %collective-permute-start.9 = (bf16[256,128]{1,0:T(8,128)(2,1)S(1)}, bf16[256,128]{1,0:T(8,128)(2,1)S(1)}, u32[]{:S(2)}, u32[]{:S(2)}) collective-permute-start(bf16[256,128]{1,0:T(8,128)(2,1)S(1)} %get-tuple-element.15), channel_id=1, source_target_pairs={{0,1},{1,2},{2,3},{3,4},{4,5},{5,6},{6,7},{7,0},{8,9},{9,10},{10,1... | collective-permute-start | bytes 196616 | tf_op jit(solution)/shard_map/ppermute | solution.py:25
  48.8 2.4 %collective-permute-start.11 = (bf16[256,128]{1,0:T(8,128)(2,1)S(1)}, bf16[256,128]{1,0:T(8,128)(2,1)S(1)}, u32[]{:S(2)}, u32[]{:S(2)}) collective-permute-start(bf16[256,128]{1,0:T(8,128)(2,1)S(1)} %get-tuple-element.13), channel_id=1, source_target_pairs={{0,7},{1,0},{2,1},{3,2},{4,3},{5,4},{6,5},{7,6},{8,15},{9,8},{10,9... | collective-permute-start | bytes 196616 | tf_op jit(solution)/shard_map/ppermute | solution.py:25
  52.0 6.6 %collective-permute-done.11 = bf16[256,128]{1,0:T(8,128)(2,1)S(1)} collective-permute-done((bf16[256,128]{1,0:T(8,128)(2,1)S(1)}, bf16[256,128]{1,0:T(8,128)(2,1)S(1)}, u32[]{:S(2)}, u32[]{:S(2)}) %collective-permute-start.11) | collective-permute-done | bytes 65568 | tf_op jit(solution)/shard_map/ppermute | solution.py:25
  58.8 2.1 %fusion.46 = f32[1152,512]{1,0:T(8,128)S(1)} fusion(f32[384,512]{1,0:T(8,128)S(1)} %bitcast_dynamic-update-slice_fusion.1, s32[384]{0:T(512)S(1)} %multiply_add_fusion), kind=kOutput, calls=%fused_computation.69 | convolution fusion | flops 2718351360 | bytes 3147264 | tf_op jit(solution)/shard_map/ts,tf->sf/dot_general | solution.py:101
  63.0 5.8 %collective-permute-start.13 = (f32[1,3,128,512]{3,2,1,0:T(8,128)S(1)}, f32[1,3,128,512]{3,2,1,0:T(8,128)S(1)}, u32[]{:S(2)}, u32[]{:S(2)}) collective-permute-start(f32[1,3,128,512]{3,2,1,0:T(8,128)S(1)} %bitcast.80), channel_id=1, source_target_pairs={{8,0},{16,8},{24,16},{32,24},{40,32},{48,40},{56,48},{64,56},{72,6... | collective-permute-start | bytes 2359304 | tf_op jit(solution)/shard_map/ppermute | solution.py:37
  68.7 7.7 %collective-permute-done.12 = f32[1,3,128,512]{3,2,1,0:T(8,128)S(1)} collective-permute-done((f32[1,3,128,512]{3,2,1,0:T(8,128)S(1)}, f32[1,3,128,512]{3,2,1,0:T(8,128)S(1)}, u32[]{:S(2)}, u32[]{:S(2)}) %collective-permute-start.12) | collective-permute-done | bytes 786464 | tf_op jit(solution)/shard_map/ppermute | solution.py:34
  82.0 5.4 %collective-permute-start.15 = (f32[5,1,128,512]{3,2,1,0:T(8,128)}, f32[5,1,128,512]{3,2,1,0:T(8,128)}, u32[]{:S(2)}, u32[]{:S(2)}) collective-permute-start(f32[5,1,128,512]{3,2,1,0:T(8,128)} %get-tuple-element.6), channel_id=1, source_target_pairs={{1,0},{2,1},{3,2},{4,3},{5,4},{6,5},{7,6},{0,7},{9,8},{10,9},{11,1... | collective-permute-start | bytes 3932168 | tf_op jit(solution)/shard_map/ppermute | solution.py:37
  90.1 5.8 %collective-permute-start.1 = (f32[1,3,128]{2,1,0:T(4,128)S(1)}, f32[1,3,128]{2,1,0:T(4,128)S(1)}, u32[]{:S(2)}, u32[]{:S(2)}) collective-permute-start(f32[1,3,128]{2,1,0:T(4,128)S(1)} %get-tuple-element.23), channel_id=1, source_target_pairs={{8,0},{16,8},{24,16},{32,24},{40,32},{48,40},{56,48},{64,56},{72,6... | collective-permute-start | bytes 4616 | tf_op jit(solution)/shard_map/ppermute | solution.py:37
  97.2 4.5 %collective-permute-start.2 = (f32[5,1,128]{2,1,0:T(1,128)S(1)}, f32[5,1,128]{2,1,0:T(1,128)S(1)}, u32[]{:S(2)}, u32[]{:S(2)}) collective-permute-start(f32[5,1,128]{2,1,0:T(1,128)S(1)} %get-tuple-element.21), channel_id=1, source_target_pairs={{0,1},{1,2},{2,3},{3,4},{4,5},{5,6},{6,7},{7,0},{8,9},{9,10},{10,1... | collective-permute-start | bytes 7688 | tf_op jit(solution)/shard_map/ppermute | solution.py:34
  101.7 3.0 %collective-permute-start.3 = (f32[5,1,128]{2,1,0:T(1,128)S(1)}, f32[5,1,128]{2,1,0:T(1,128)S(1)}, u32[]{:S(2)}, u32[]{:S(2)}) collective-permute-start(f32[5,1,128]{2,1,0:T(1,128)S(1)} %get-tuple-element.22), channel_id=1, source_target_pairs={{1,0},{2,1},{3,2},{4,3},{5,4},{6,5},{7,6},{0,7},{9,8},{10,9},{11,1... | collective-permute-start | bytes 7688 | tf_op jit(solution)/shard_map/ppermute | solution.py:37
  104.7 35.0 %collective-permute-done.2 = f32[5,1,128]{2,1,0:T(1,128)S(1)} collective-permute-done((f32[5,1,128]{2,1,0:T(1,128)S(1)}, f32[5,1,128]{2,1,0:T(1,128)S(1)}, u32[]{:S(2)}, u32[]{:S(2)}) %collective-permute-start.2) | collective-permute-done | bytes 2592 | tf_op jit(solution)/shard_map/ppermute | solution.py:34
  140.0 2.3 %pad_maximum_fusion = f32[5,5,128,512]{3,2,1,0:T(8,128)S(1)} fusion(f32[5,1,128,512]{3,2,1,0:T(8,128)} %collective-permute-done.15, f32[1,3,128,512]{3,2,1,0:T(8,128)} %copy-done, f32[3,3,128,512]{3,2,1,0:T(8,128)S(1)} %bitcast.75, f32[1,3,128,512]{3,2,1,0:T(8,128)S(1)} %collective-permute-done.12, f32[5,1,128,512]{3,2,1,0:T(8,128)} %collective-permute-done.14), kind=kLoop, calls=%fused_computation | loop fusion | flops 6553600 | bytes 13107200 | tf_op jit(solution)/shard_map/concatenate | solution.py:38
  142.6 5.8 %fusion = f32[1024,512]{1,0:T(8,128)} fusion(f32[1152,512]{1,0:T(8,128)S(1)} %bitcast.77, s32[1152]{0:T(1024)S(1)} %convert_element_type.39), kind=kOutput, calls=%fused_computation.2 | convolution fusion | flops 7248936960 | bytes 4461056 | tf_op jit(solution)/shard_map/sc,sf->cf/dot_general | solution.py:115
  153.9 5.8 %collective-permute-start.17 = (f32[4,32,4,128]{3,2,1,0:T(4,128)S(1)}, f32[4,32,4,128]{3,2,1,0:T(4,128)S(1)}, u32[]{:S(2)}, u32[]{:S(2)}) collective-permute-start(f32[4,32,4,128]{3,2,1,0:T(4,128)S(1)} %bitcast.86), channel_id=1, source_target_pairs={{8,0},{16,8},{24,16},{32,24},{40,32},{48,40},{56,48},{64,56},{72,6... | collective-permute-start | bytes 786440 | tf_op jit(solution)/shard_map/ppermute | solution.py:37
  163.5 5.3 %fusion.25 = f32[32,32,4,128]{3,2,1,0:T(4,128)S(1)} fusion(f32[4,32,4,128]{3,2,1,0:T(4,128)S(1)} %collective-permute-done.17, f32[4,32,4,128]{3,2,1,0:T(4,128)S(1)} %collective-permute-done.16, f32[32,32,4,128]{3,2,1,0:T(4,128)S(1)} %bitcast.76), kind=kLoop, calls=%fused_computation.39 | loop fusion | flops 13107200 | bytes 4718592 | tf_op jit(solution)/shard_map/add | solution.py:134
  168.9 4.3 %collective-permute-start.18 = (f32[32,4,4,128]{3,2,1,0:T(4,128)S(1)}, f32[32,4,4,128]{3,2,1,0:T(4,128)S(1)}, u32[]{:S(2)}, u32[]{:S(2)}) collective-permute-start(f32[32,4,4,128]{3,2,1,0:T(4,128)S(1)} %get-tuple-element.9), channel_id=1, source_target_pairs={{0,1},{1,2},{2,3},{3,4},{4,5},{5,6},{6,7},{7,0},{8,9},{9,10},{10,1... | collective-permute-start | bytes 786440 | tf_op jit(solution)/shard_map/ppermute | solution.py:34
  173.2 3.0 %collective-permute-start.19 = (f32[32,4,4,128]{3,2,1,0:T(4,128)S(1)}, f32[32,4,4,128]{3,2,1,0:T(4,128)S(1)}, u32[]{:S(2)}, u32[]{:S(2)}) collective-permute-start(f32[32,4,4,128]{3,2,1,0:T(4,128)S(1)} %get-tuple-element.10), channel_id=1, source_target_pairs={{1,0},{2,1},{3,2},{4,3},{5,4},{6,5},{7,6},{0,7},{9,8},{10,9},{11,1... | collective-permute-start | bytes 786440 | tf_op jit(solution)/shard_map/ppermute | solution.py:37
  176.2 3.4 %collective-permute-done.18 = f32[32,4,4,128]{3,2,1,0:T(4,128)S(1)} collective-permute-done((f32[32,4,4,128]{3,2,1,0:T(4,128)S(1)}, f32[32,4,4,128]{3,2,1,0:T(4,128)S(1)}, u32[]{:S(2)}, u32[]{:S(2)}) %collective-permute-start.18) | collective-permute-done | bytes 262176 | tf_op jit(solution)/shard_map/ppermute | solution.py:34
  179.6 5.5 %collective-permute-done.19 = f32[32,4,4,128]{3,2,1,0:T(4,128)S(1)} collective-permute-done((f32[32,4,4,128]{3,2,1,0:T(4,128)S(1)}, f32[32,4,4,128]{3,2,1,0:T(4,128)S(1)}, u32[]{:S(2)}, u32[]{:S(2)}) %collective-permute-start.19) | collective-permute-done | bytes 262176 | tf_op jit(solution)/shard_map/ppermute | solution.py:37
  185.1 5.7 %fusion.5 = f32[32,32,4,128]{3,2,1,0:T(4,128)} fusion(f32[32,4,4,128]{3,2,1,0:T(4,128)S(1)} %collective-permute-done.19, f32[32,4,4,128]{3,2,1,0:T(4,128)S(1)} %collective-permute-done.18, f32[32,32,4,128]{3,2,1,0:T(4,128)S(1)} %fusion.25), kind=kLoop, calls=%fused_computation.19 | loop fusion | flops 13107200 | bytes 4718592 | tf_op jit(solution)/shard_map/add | solution.py:138
  (83 shorter events, 38.0 us)
Async XLA Ops:
  0.0 39.9 %copy-start.1 = (bf16[1,1,2048,128]{3,2,1,0:T(8,128)(2,1)S(1)}, bf16[1,1,2048,128]{3,2,1,0:T(8,128)(2,1)}, u32[]{:S(2)}) copy-start(bf16[1,1,2048,128]{3,2,1,0:T(8,128)(2,1)} %param.6) | copy-start | bytes 1572868
  0.0 40.4 %copy-start.2 = (s32[1,1,384,1]{2,3,1,0:T(1,128)S(1)}, s32[1,1,384,1]{2,3,1,0:T(1,128)}, u32[]{:S(2)}) copy-start(s32[1,1,384,1]{2,3,1,0:T(1,128)} %param.8) | copy-start | bytes 4612
  14.8 27.0 %collective-permute-start.4 = (bf16[4,256]{1,0:T(4,128)(2,1)S(1)}, bf16[4,256]{1,0:T(4,128)(2,1)S(1)}, u32[]{:S(2)}, u32[]{:S(2)}) collective-permute-start(bf16[4,256]{1,0:T(4,128)(2,1)S(1)} %get-tuple-element.20), channel_id=1, source_target_pairs={{0,8},{8,16},{16,24},{24,32},{32,40},{40,48},{48,56},{56,64},{64,7... | collective-permute-start | bytes 6152 | tf_op jit(solution)/shard_map/ppermute | solution.py:25
  17.8 33.7 %collective-permute-start.5 = (bf16[256,128]{1,0:T(8,128)(2,1)S(1)}, bf16[256,128]{1,0:T(8,128)(2,1)S(1)}, u32[]{:S(2)}, u32[]{:S(2)}) collective-permute-start(bf16[256,128]{1,0:T(8,128)(2,1)S(1)} %get-tuple-element.16), channel_id=1, source_target_pairs={{0,8},{8,16},{16,24},{24,32},{32,40},{40,48},{48,56},{56,64},{64,7... | collective-permute-start | bytes 196616 | tf_op jit(solution)/shard_map/ppermute | solution.py:25
  21.7 22.1 %collective-permute-start.6 = (bf16[4,256]{1,0:T(4,128)(2,1)S(1)}, bf16[4,256]{1,0:T(4,128)(2,1)S(1)}, u32[]{:S(2)}, u32[]{:S(2)}) collective-permute-start(bf16[4,256]{1,0:T(4,128)(2,1)S(1)} %get-tuple-element.18), channel_id=1, source_target_pairs={{0,504},{8,0},{16,8},{24,16},{32,24},{40,32},{48,40},{56,48},{64,5... | collective-permute-start | bytes 6152 | tf_op jit(solution)/shard_map/ppermute | solution.py:25
  30.9 18.0 %collective-permute-start.8 = (bf16[4,256]{1,0:T(4,128)(2,1)S(1)}, bf16[4,256]{1,0:T(4,128)(2,1)S(1)}, u32[]{:S(2)}, u32[]{:S(2)}) collective-permute-start(bf16[4,256]{1,0:T(4,128)(2,1)S(1)} %get-tuple-element.19), channel_id=1, source_target_pairs={{0,1},{1,2},{2,3},{3,4},{4,5},{5,6},{6,7},{7,0},{8,9},{9,10},{10,1... | collective-permute-start | bytes 6152 | tf_op jit(solution)/shard_map/ppermute | solution.py:25
  33.5 17.9 %collective-permute-start.10 = (bf16[4,256]{1,0:T(4,128)(2,1)S(1)}, bf16[4,256]{1,0:T(4,128)(2,1)S(1)}, u32[]{:S(2)}, u32[]{:S(2)}) collective-permute-start(bf16[4,256]{1,0:T(4,128)(2,1)S(1)} %get-tuple-element.17), channel_id=1, source_target_pairs={{0,7},{1,0},{2,1},{3,2},{4,3},{5,4},{6,5},{7,6},{8,15},{9,8},{10,9... | collective-permute-start | bytes 6152 | tf_op jit(solution)/shard_map/ppermute | solution.py:25
  41.7 9.9 %collective-permute-start.7 = (bf16[256,128]{1,0:T(8,128)(2,1)S(1)}, bf16[256,128]{1,0:T(8,128)(2,1)S(1)}, u32[]{:S(2)}, u32[]{:S(2)}) collective-permute-start(bf16[256,128]{1,0:T(8,128)(2,1)S(1)} %get-tuple-element.14), channel_id=1, source_target_pairs={{0,504},{8,0},{16,8},{24,16},{32,24},{40,32},{48,40},{56,48},{64,5... | collective-permute-start | bytes 196616 | tf_op jit(solution)/shard_map/ppermute | solution.py:25
  43.8 8.0 %collective-permute-start.9 = (bf16[256,128]{1,0:T(8,128)(2,1)S(1)}, bf16[256,128]{1,0:T(8,128)(2,1)S(1)}, u32[]{:S(2)}, u32[]{:S(2)}) collective-permute-start(bf16[256,128]{1,0:T(8,128)(2,1)S(1)} %get-tuple-element.15), channel_id=1, source_target_pairs={{0,1},{1,2},{2,3},{3,4},{4,5},{5,6},{6,7},{7,0},{8,9},{9,10},{10,1... | collective-permute-start | bytes 196616 | tf_op jit(solution)/shard_map/ppermute | solution.py:25
  48.8 9.8 %collective-permute-start.11 = (bf16[256,128]{1,0:T(8,128)(2,1)S(1)}, bf16[256,128]{1,0:T(8,128)(2,1)S(1)}, u32[]{:S(2)}, u32[]{:S(2)}) collective-permute-start(bf16[256,128]{1,0:T(8,128)(2,1)S(1)} %get-tuple-element.13), channel_id=1, source_target_pairs={{0,7},{1,0},{2,1},{3,2},{4,3},{5,4},{6,5},{7,6},{8,15},{9,8},{10,9... | collective-permute-start | bytes 196616 | tf_op jit(solution)/shard_map/ppermute | solution.py:25
  61.1 15.4 %collective-permute-start.12 = (f32[1,3,128,512]{3,2,1,0:T(8,128)S(1)}, f32[1,3,128,512]{3,2,1,0:T(8,128)S(1)}, u32[]{:S(2)}, u32[]{:S(2)}) collective-permute-start(f32[1,3,128,512]{3,2,1,0:T(8,128)S(1)} %bitcast.81), channel_id=1, source_target_pairs={{0,8},{8,16},{16,24},{24,32},{32,40},{40,48},{48,56},{56,64},{64,7... | collective-permute-start | bytes 2359304 | tf_op jit(solution)/shard_map/ppermute | solution.py:34
  63.0 15.2 %collective-permute-start.13 = (f32[1,3,128,512]{3,2,1,0:T(8,128)S(1)}, f32[1,3,128,512]{3,2,1,0:T(8,128)S(1)}, u32[]{:S(2)}, u32[]{:S(2)}) collective-permute-start(f32[1,3,128,512]{3,2,1,0:T(8,128)S(1)} %bitcast.80), channel_id=1, source_target_pairs={{8,0},{16,8},{24,16},{32,24},{40,32},{48,40},{56,48},{64,56},{72,6... | collective-permute-start | bytes 2359304 | tf_op jit(solution)/shard_map/ppermute | solution.py:37
  78.2 1.9 copy-start
  78.2 9.2 %copy-start.3 = (s32[1,1,384]{2,1,0:T(1,128)S(1)}, s32[1,1,384]{2,1,0:T(1,128)}, u32[]{:S(2)}) copy-start(s32[1,1,384]{2,1,0:T(1,128)} %param.9) | copy-start | bytes 4612
  80.1 59.8 %collective-permute-start.14 = (f32[5,1,128,512]{3,2,1,0:T(8,128)}, f32[5,1,128,512]{3,2,1,0:T(8,128)}, u32[]{:S(2)}, u32[]{:S(2)}) collective-permute-start(f32[5,1,128,512]{3,2,1,0:T(8,128)} %get-tuple-element.5), channel_id=1, source_target_pairs={{0,1},{1,2},{2,3},{3,4},{4,5},{5,6},{6,7},{7,0},{8,9},{9,10},{10,1... | collective-permute-start | bytes 3932168 | tf_op jit(solution)/shard_map/ppermute | solution.py:34
  82.0 57.9 %collective-permute-start.15 = (f32[5,1,128,512]{3,2,1,0:T(8,128)}, f32[5,1,128,512]{3,2,1,0:T(8,128)}, u32[]{:S(2)}, u32[]{:S(2)}) collective-permute-start(f32[5,1,128,512]{3,2,1,0:T(8,128)} %get-tuple-element.6), channel_id=1, source_target_pairs={{1,0},{2,1},{3,2},{4,3},{5,4},{6,5},{7,6},{0,7},{9,8},{10,9},{11,1... | collective-permute-start | bytes 3932168 | tf_op jit(solution)/shard_map/ppermute | solution.py:37
  88.2 7.7 %collective-permute-start = (f32[1,3,128]{2,1,0:T(4,128)S(1)}, f32[1,3,128]{2,1,0:T(4,128)S(1)}, u32[]{:S(2)}, u32[]{:S(2)}) collective-permute-start(f32[1,3,128]{2,1,0:T(4,128)S(1)} %get-tuple-element.24), channel_id=1, source_target_pairs={{0,8},{8,16},{16,24},{24,32},{32,40},{40,48},{48,56},{56,64},{64,7... | collective-permute-start | bytes 4616 | tf_op jit(solution)/shard_map/ppermute | solution.py:34
  90.1 7.0 %collective-permute-start.1 = (f32[1,3,128]{2,1,0:T(4,128)S(1)}, f32[1,3,128]{2,1,0:T(4,128)S(1)}, u32[]{:S(2)}, u32[]{:S(2)}) collective-permute-start(f32[1,3,128]{2,1,0:T(4,128)S(1)} %get-tuple-element.23), channel_id=1, source_target_pairs={{8,0},{16,8},{24,16},{32,24},{40,32},{48,40},{56,48},{64,56},{72,6... | collective-permute-start | bytes 4616 | tf_op jit(solution)/shard_map/ppermute | solution.py:37
  97.2 42.5 %collective-permute-start.2 = (f32[5,1,128]{2,1,0:T(1,128)S(1)}, f32[5,1,128]{2,1,0:T(1,128)S(1)}, u32[]{:S(2)}, u32[]{:S(2)}) collective-permute-start(f32[5,1,128]{2,1,0:T(1,128)S(1)} %get-tuple-element.21), channel_id=1, source_target_pairs={{0,1},{1,2},{2,3},{3,4},{4,5},{5,6},{6,7},{7,0},{8,9},{9,10},{10,1... | collective-permute-start | bytes 7688 | tf_op jit(solution)/shard_map/ppermute | solution.py:34
  101.7 38.0 %collective-permute-start.3 = (f32[5,1,128]{2,1,0:T(1,128)S(1)}, f32[5,1,128]{2,1,0:T(1,128)S(1)}, u32[]{:S(2)}, u32[]{:S(2)}) collective-permute-start(f32[5,1,128]{2,1,0:T(1,128)S(1)} %get-tuple-element.22), channel_id=1, source_target_pairs={{1,0},{2,1},{3,2},{4,3},{5,4},{6,5},{7,6},{0,7},{9,8},{10,9},{11,1... | collective-permute-start | bytes 7688 | tf_op jit(solution)/shard_map/ppermute | solution.py:37
  152.0 9.8 %collective-permute-start.16 = (f32[4,32,4,128]{3,2,1,0:T(4,128)S(1)}, f32[4,32,4,128]{3,2,1,0:T(4,128)S(1)}, u32[]{:S(2)}, u32[]{:S(2)}) collective-permute-start(f32[4,32,4,128]{3,2,1,0:T(4,128)S(1)} %bitcast.87), channel_id=1, source_target_pairs={{0,8},{8,16},{16,24},{24,32},{32,40},{40,48},{48,56},{56,64},{64,7... | collective-permute-start | bytes 786440 | tf_op jit(solution)/shard_map/ppermute | solution.py:34
  153.9 9.6 %collective-permute-start.17 = (f32[4,32,4,128]{3,2,1,0:T(4,128)S(1)}, f32[4,32,4,128]{3,2,1,0:T(4,128)S(1)}, u32[]{:S(2)}, u32[]{:S(2)}) collective-permute-start(f32[4,32,4,128]{3,2,1,0:T(4,128)S(1)} %bitcast.86), channel_id=1, source_target_pairs={{8,0},{16,8},{24,16},{32,24},{40,32},{48,40},{56,48},{64,56},{72,6... | collective-permute-start | bytes 786440 | tf_op jit(solution)/shard_map/ppermute | solution.py:37
  168.9 10.7 %collective-permute-start.18 = (f32[32,4,4,128]{3,2,1,0:T(4,128)S(1)}, f32[32,4,4,128]{3,2,1,0:T(4,128)S(1)}, u32[]{:S(2)}, u32[]{:S(2)}) collective-permute-start(f32[32,4,4,128]{3,2,1,0:T(4,128)S(1)} %get-tuple-element.9), channel_id=1, source_target_pairs={{0,1},{1,2},{2,3},{3,4},{4,5},{5,6},{6,7},{7,0},{8,9},{9,10},{10,1... | collective-permute-start | bytes 786440 | tf_op jit(solution)/shard_map/ppermute | solution.py:34
  173.2 11.9 %collective-permute-start.19 = (f32[32,4,4,128]{3,2,1,0:T(4,128)S(1)}, f32[32,4,4,128]{3,2,1,0:T(4,128)S(1)}, u32[]{:S(2)}, u32[]{:S(2)}) collective-permute-start(f32[32,4,4,128]{3,2,1,0:T(4,128)S(1)} %get-tuple-element.10), channel_id=1, source_target_pairs={{1,0},{2,1},{3,2},{4,3},{5,4},{6,5},{7,6},{0,7},{9,8},{10,9},{11,1... | collective-permute-start | bytes 786440 | tf_op jit(solution)/shard_map/ppermute | solution.py:37
where the time goes:
time: 192 us; the launch traced here: 191 us
  starting transfers between devices  76.8 us (40%)
  waiting for transfers between devices  65.1 us (34%)
  other arithmetic  21.8 us (11%)
  matrix products  11.6 us (6%)
  between operations  8.06 us (4%)
  local copies, waits for them, and re-layouts  7.35 us (4%)
    ppermute x6, waiting for transfers between devices, padded(): lax.ppermute(lax.slice_in_dim(block, block.shape[dim] - width, None, axis...  48.2 us
    ppermute x8, starting transfers between devices, passed_along(): return lax.ppermute(value, axis, pairs)  31.6 us
    ppermute x6, starting transfers between devices, padded(): lax.ppermute(lax.slice_in_dim(block, 0, width, axis=dim), axis, backward)  28.7 us
    ppermute x6, starting transfers between devices, padded(): lax.ppermute(lax.slice_in_dim(block, block.shape[dim] - width, None, axis...  16.5 us
    ppermute x6, waiting for transfers between devices, padded(): lax.ppermute(lax.slice_in_dim(block, 0, width, axis=dim), axis, backward)  10.2 us
    ppermute x8, waiting for transfers between devices, passed_along(): return lax.ppermute(value, axis, pairs)  6.6 us
    dot_general x1, matrix products, local(): jnp.einsum('sc,sf->cf', column_hits, got_tiles, precision=lax.Precision.H...  5.8 us
    add x1, other arithmetic, local(): filtered + gauss_weights[tap_index] * widened_z[:, tap_index:tap_index + CZ]  5.66 us
  transfers between devices with their start and end apart: 20, of which 9 were waited for; matrix products, arithmetic and copies ran while one was open for 3% of the time, Pallas kernels for 0%

commit v1 on v0

v1 whole, which is shorter than its diff:
```python
import math

import jax
import jax.numpy as jnp
from jax import lax
from jax.experimental import pallas as pl
from jax.experimental.pallas import tpu as pltpu
from jax.sharding import PartitionSpec as P

CX = 32
CZ = 32
NY = 128
CH = 4
P_SIZE = 2048
G = 8
REACH = 4
M = 256
KT = 128
NT = 384
F = CH * NY
COLS = CX * CZ
MESH = pl.DeviceIdType.MESH
f32, bf16, i32 = jnp.float32, jnp.bfloat16, jnp.int32
HIGHEST = lax.Precision.HIGHEST


def gauss_taps():
    raw_values = [math.exp(-k * k / 8.0) for k in range(-REACH, REACH + 1)]
    total = sum(raw_values)
    return [v / total for v in raw_values]


TAPS = gauss_taps()


def iota(shape, dim):
    return lax.broadcasted_iota(i32, shape, dim)


def eye():
    return iota((128, 128), 0) == iota((128, 128), 1)


def to_row(column):
    same = eye()
    return [
        jnp.sum(jnp.where(same, column[i : i + 128], 0.0), axis=0, keepdims=True)
        for i in range(0, column.shape[0], 128)
    ]


def to_column(row):
    return jnp.sum(jnp.where(eye(), row, 0.0), axis=1, keepdims=True)


def coded(rows):
    top = jnp.maximum(jnp.max(jnp.abs(rows), axis=1, keepdims=True), 1e-30)
    exponent = jnp.ceil(jnp.log2(top)) - 15.0
    q = jnp.floor(rows * jnp.exp2(-exponent) + 0.5)
    q = jnp.clip(q, -32767.0, 32767.0).astype(i32)
    return (q[:, : F // 2] << 16) | (q[:, F // 2 :] & 0xFFFF), exponent


def integers(packed):
    return jnp.concatenate([packed >> 16, (packed << 16) >> 16], axis=1)


def halves(packed):
    q = integers(packed)
    return (q >> 8).astype(f32).astype(bf16), (q & 255).astype(f32).astype(bf16)


def info_rows(*rows):
    row_id = iota((8, 128), 0)
    block = jnp.zeros((8, 128), i32)
    for i, row in enumerate(rows):
        block = jnp.where(row_id == i, row.astype(i32), block)
    return jnp.concatenate([block, jnp.zeros((8, 128), i32)], axis=1)


def kernel(
    cnt, drag_ref, w_ref, own_ref, col_ref, out_ref,
    lhs, dragk, tf, mo, mr, ls, lr, plc, u, xs, xr, hl, rhs, sx, edge, hx, hxr, hz, hzr, hcr, zx, ax,
    m_s, m_r, t_s, t_r, x_s, x_r, hx_s, hx_r, hz_s, hz_r, hc_s, hc_r,
):
    na, nb = lax.axis_size("gx"), lax.axis_size("gz")
    a, b = lax.axis_index("gx"), lax.axis_index("gz")
    a_up, a_dn = lax.rem(a + 1, na), lax.rem(a + na - 1, na)
    b_up, b_dn = lax.rem(b + 1, nb), lax.rem(b + nb - 1, nb)
    odd = lax.rem(b, 2)
    flip = b + 1 - 2 * odd
    b_up2, b_dn2 = lax.rem(b + 2, nb), lax.rem(b + nb - 2, nb)
    relay = jnp.where(odd == 0, b_up2, b_dn2)
    sides_x = ((a_up, b), (a_dn, b))
    sides_z = ((a, b_up), (a, b_dn))
    barrier = pltpu.get_barrier_semaphore()
    for other in sides_x + sides_z + ((a, b_up2), (a, b_dn2)):
        pl.semaphore_signal(barrier, inc=1, device_id=other, device_id_type=MESH)

    def send(src, dst, s_sem, r_sem, to):
        copy = pltpu.make_async_remote_copy(
            src_ref=src, dst_ref=dst, send_sem=s_sem, recv_sem=r_sem,
            device_id=to, device_id_type=MESH,
        )
        copy.start()
        return copy

    gap = iota((NY, NY), 0) - iota((NY, NY), 1)
    band = jnp.zeros((NY, NY), f32)
    for k in range(2 * REACH + 1):
        band = jnp.where(gap == k - REACH, TAPS[k], band)

    def along_y(rows):
        return jnp.dot(rows, band, precision=HIGHEST, preferred_element_type=f32)

    slot = iota((1, P_SIZE), 1)
    drag = drag_ref[...].astype(f32)
    t_id = iota((32, P_SIZE), 0)
    starts, total = [], cnt[0, 0]
    for d in range(4):
        starts.append(total)
        total = total + cnt[0, d + 1]
    for d in range(4):
        rel = slot - starts[d]
        group = jnp.where((rel >= 0) & (rel < cnt[0, d + 1]), rel >> 3, -1)
        mask = group == t_id
        for c in range(CH):
            lhs[d * 128 + c * 32 : d * 128 + c * 32 + 32, :] = jnp.where(
                mask, drag[c : c + 1, :], 0.0
            ).astype(bf16)
    moved = along_y(jnp.dot(lhs[...], w_ref[...], preferred_element_type=f32))
    for d in range(4):
        for c in range(CH):
            tf[d * 32 : d * 32 + 32, c * NY : (c + 1) * NY] = moved[
                d * 128 + c * 32 : d * 128 + c * 32 + 32, :
            ]
    v, e = coded(tf[0:128, :])
    info = info_rows(to_row(e)[0])
    for d in range(4):
        mo[d, 0:32, :] = v[d * 32 : d * 32 + 32, :]
        mo[d, 32:40, :] = info
    pl.semaphore_wait(barrier, 6)
    copies = []
    for d, to in ((2, sides_z[0]), (3, sides_z[1]), (0, sides_x[0]), (1, sides_x[1])):
        copies.append(send(mo.at[d], mr.at[d], m_s.at[d], m_r.at[d], to))
    m_copies = list(copies)

    dragk[...] = jnp.where(slot < cnt[0, 0], drag, 0.0)
    near = (iota((32, 256), 1) >> 3) == iota((32, 256), 0)
    own_codes, own_cols = own_ref[...], col_ref[...]
    list_copies = []

    def ship(i):
        copy = send(ls.at[i], lr.at[0, i], t_s.at[0, i], t_r.at[0, i], (a, flip))
        copies.append(copy)
        list_copies.append(copy)

    for half in range(2):
        for g in range(4 * half, 4 * half + 4):
            part = dragk[:, g * 256 : (g + 1) * 256]
            rows = jnp.concatenate(
                [jnp.where(near, part[c : c + 1, :], 0.0) for c in range(CH)], axis=0
            )
            made = along_y(
                jnp.dot(
                    rows.astype(bf16), w_ref[g * 256 : (g + 1) * 256, :], preferred_element_type=f32
                )
            )
            for c in range(CH):
                tf[g * 32 : g * 32 + 32, c * NY : (c + 1) * NY] = made[c * 32 : c * 32 + 32, :]
        at = half * 128
        v, e = coded(tf[at : at + 128, :])
        ls[half, 0:128, :] = v
        ls[half, 128:136, :] = info_rows(
            own_codes[:, at : at + 128], own_cols[:, at : at + 128], to_row(e)[0]
        )
        ship(half)

    lane = iota((1, 128), 1)
    e_row = jnp.zeros((1, 128), i32)
    for d in (0, 1, 2, 3):
        m_copies[{2: 0, 3: 1, 0: 2, 1: 3}[d]].wait_recv()
        ls[2, d * 32 : d * 32 + 32, :] = mr[d, 0:32, :]
        e_row = jnp.where((lane >> 5) == d, mr[d, 32:33, 0:128], e_row)
    ls[2, 128:136, :] = info_rows(own_codes[:, 256:384], own_cols[:, 256:384], e_row)
    ship(2)

    before = (iota((NT, NT), 0) < iota((NT, NT), 1)).astype(f32).astype(bf16)
    slot_id = iota((KT, NT), 0).astype(f32)
    sub = iota((8, 128), 0)
    sub3 = iota((8, NT), 0)

    def compact(j, chunk, step_z):
        infos = [chunk(i)[128:136, 0:128] for i in range(3)]
        codes = jnp.concatenate([p[0:1] for p in infos], axis=1)
        cols = jnp.concatenate([p[1:2] for p in infos], axis=1)
        exps = jnp.concatenate([p[2:3] for p in infos], axis=1)
        hit = (codes == 3 * sub3 + 1 + step_z) & (sub3 < 3)
        ranks = jnp.dot(hit.astype(f32).astype(bf16), before, preferred_element_type=f32)
        pos = jnp.where(hit, ranks, -1.0)
        for s in range(3):
            plc[s * KT : (s + 1) * KT, :] = (
                (pos[s : s + 1, :] == slot_id).astype(f32).astype(bf16)
            )
        for i in range(3):
            hi, lo = halves(chunk(i)[0:128, :])
            u[i * 128 : (i + 1) * 128, 0:F] = hi
            u[i * 128 : (i + 1) * 128, F : 2 * F] = lo
        fields = jnp.zeros((8, NT), f32)
        for i, row in enumerate((cols >> 5, cols & 31, exps, jnp.ones((1, NT), i32))):
            fields = jnp.where(sub3 == i, row.astype(f32), fields)
        got = lax.dot_general(
            fields.astype(bf16), plc[...], (((1,), (1,)), ((), ())), preferred_element_type=f32
        )
        col_f = got[0:1] * 32.0 + got[1:2] - jnp.where(got[3:4] > 0.5, 0.0, 1.0)
        exp_f = got[2:3]
        for n, s in ((0, 2), (1, 0)):
            out = jnp.dot(
                plc[s * KT : (s + 1) * KT, :], u[...], preferred_element_type=f32
            ).astype(i32)
            q = (out[:, 0:F] << 8) + out[:, F : 2 * F]
            xs[n, j, 0:128, :] = (q[:, : F // 2] << 16) | (q[:, F // 2 :] & 0xFFFF)
            xs[n, j, 128:136, :] = info_rows(
                col_f[:, s * KT : (s + 1) * KT], exp_f[:, s * KT : (s + 1) * KT]
            )
            x_copies[n, j] = send(
                xs.at[n, j], xr.at[n, j], x_s.at[n, j], x_r.at[n, j], sides_x[n]
            )
            copies.append(x_copies[n, j])
        mid = jnp.dot(plc[KT : 2 * KT, :], u[...], preferred_element_type=f32).astype(bf16)
        rhs[0:128, :] = mid[:, 0:F]
        rhs[128:256, :] = mid[:, F : 2 * F]
        one_hot(0, col_f[:, KT : 2 * KT], exp_f[:, KT : 2 * KT])

    x_copies = {}
    row_id = iota((COLS + 256, 128), 0)
    edge_id = row_id - COLS
    edge_col = ((edge_id & 127) >> 2) * CZ + (edge_id & 3) + jnp.where(edge_id >= 128, CZ - REACH, 0)
    row_col = jnp.where(row_id < COLS, row_id, edge_col).astype(f32)

    def one_hot(slot_at, col_f, exp_f):
        scale = jnp.exp2(exp_f)
        h = jnp.where(row_col == col_f, scale, 0.0)
        hl[:, slot_at * 256 : slot_at * 256 + 128] = (h * 256.0).astype(bf16)
        hl[:, slot_at * 256 + 128 : slot_at * 256 + 256] = h.astype(bf16)

    def deposit(j):
        for n in range(2):
            x_copies[n, j].wait_recv()
            at = 256 * (n + 1)
            hi, lo = halves(xr[n, j, 0:128, :])
            rhs[at : at + 128, :] = hi
            rhs[at + 128 : at + 256, :] = lo
            got = xr[n, j, 128:136, 0:128].astype(f32)
            one_hot(n + 1, got[0:1], got[1:2])
        for i in range(5):
            part = jnp.dot(
                hl[i * 256 : (i + 1) * 256, :], rhs[...], preferred_element_type=f32
            )
            if i < 4:
                at = 128 + i * 256
                if j:
                    part = part + sx[at : at + 256, :]
                sx[at : at + 256, :] = part
            else:
                if j:
                    part = part + edge[...]
                edge[...] = part

    toward = jnp.where(odd == 0, -1, 1)
    compact(0, lambda i: ls[i], 0)
    relay_copies = []
    for i in range(3):
        list_copies[i].wait_recv()
        copy = send(lr.at[0, i], lr.at[1, i], t_s.at[1, i], t_r.at[1, i], (a, relay))
        copies.append(copy)
        relay_copies.append(copy)
    deposit(0)
    compact(1, lambda i: lr[0, i], toward)
    deposit(1)
    for i in range(3):
        relay_copies[i].wait_recv()
    compact(2, lambda i: lr[1, i], -toward)
    deposit(2)

    ve, ee = coded(edge[...])
    ee_rows = to_row(ee)
    z_copies = []
    for n, s in ((0, 1), (1, 0)):
        hz[n, 0:128, :] = ve[s * 128 : (s + 1) * 128, :]
        hz[n, 128:136, :] = info_rows(ee_rows[s])
        z_copies.append(send(hz.at[n], hzr.at[n], hz_s.at[n], hz_r.at[n], sides_z[n]))
    h_copies = []
    for n in range(2):
        at = COLS if n == 0 else 128
        vx, ex = coded(sx[at : at + 128, :])
        hx[n, 0:128, :] = vx
        here = 112 if n == 0 else 0
        hx[n, 128:144, :] = ve[here : here + 16, :]
        hx[n, 144:152, :] = info_rows(to_row(ex)[0], ee_rows[0], ee_rows[1])
        hx[n, 152:168, :] = ve[128 + here : 128 + here + 16, :]
        h_copies.append(send(hx.at[n], hxr.at[n], hx_s.at[n], hx_r.at[n], sides_x[n]))
    copies += z_copies + h_copies
    c_copies = []
    for n in range(2):
        h_copies[n].wait_recv()
        for m in range(2):
            at = 144 if m == 0 else 128
            copy = send(
                hxr.at[n, pl.ds(at, 24)], hcr.at[n, m], hc_s.at[n, m], hc_r.at[n, m], sides_z[m]
            )
            c_copies.append(copy)
    copies += c_copies
    for n in range(2):
        got = hxr[n, 0:128, :]
        scale = jnp.exp2(to_column(hxr[n, 144:145, 0:128].astype(f32)))
        at = 0 if n == 0 else COLS + 128
        sx[at : at + 128, :] = integers(got).astype(f32) * scale

    EXT = (CZ + 2 * REACH) * CH

    def x_pass(x, _):
        total = None
        for k in range(2 * REACH + 1):
            at = pl.multiple_of((x + k) * CZ, CZ)
            term = sx[pl.ds(at, CZ), :] * TAPS[k]
            total = term if total is None else total + term
        for c in range(CH):
            ax[pl.ds(x * EXT + 4 * CH + c, CZ, stride=CH), :] = total[:, c * NY : (c + 1) * NY]
        return 0

    lax.fori_loop(0, CX, x_pass, 0)

    for n in range(2):
        z_copies[n].wait_recv()
    for copy in c_copies:
        copy.wait_recv()
    for n in range(2):
        scale = jnp.exp2(to_column(hzr[n, 128:129, 0:128].astype(f32)))
        main = integers(hzr[n, 0:128, :]).astype(f32) * scale
        for c in range(CH):
            zx[n, pl.ds(4 * 4 * CH + c, 128, stride=CH), :] = main[:, c * NY : (c + 1) * NY]
        for m in range(2):
            data_at, info_at = (8, 0) if n == 0 else (0, 16)
            e_corner = hcr[m, n, info_at + (2 if n == 0 else 1) : info_at + (3 if n == 0 else 2), 0:128]
            col = jnp.exp2(to_column(e_corner.astype(f32)))
            here = 112 if m == 0 else 0
            corner = integers(hcr[m, n, data_at : data_at + 16, :]).astype(f32) * col[here : here + 16]
            base = 0 if m == 0 else (CX + REACH) * 4 * CH
            for c in range(CH):
                zx[n, pl.ds(base + c, 16, stride=CH), :] = corner[:, c * NY : (c + 1) * NY]

    def z_pass(x, _):
        for n in range(2):
            total = None
            for k in range(2 * REACH + 1):
                at = pl.multiple_of((x + k) * 4 * CH, 4 * CH)
                term = zx[n, pl.ds(at, 4 * CH), :] * TAPS[k]
                total = term if total is None else total + term
            at = x * EXT + (0 if n == 0 else (CZ + REACH) * CH)
            ax[pl.ds(pl.multiple_of(at, 8), 4 * CH), :] = total
        total = None
        for k in range(2 * REACH + 1):
            term = ax[pl.ds(x * EXT + CH * k, CZ * CH), :] * TAPS[k]
            total = term if total is None else total + term
        out_ref[pl.ds(pl.multiple_of(x * CZ * CH, CZ * CH), CZ * CH), :] = total
        return 0

    lax.fori_loop(0, CX, z_pass, 0)
    for copy in copies:
        copy.wait_send()


def local(particle_drag, particle_weights, migration_counts, tile_owner, tile_column):
    vmem = pl.BlockSpec(memory_space=pltpu.VMEM)
    dma = pltpu.SemaphoreType.DMA
    out = pl.pallas_call(
        kernel,
        out_shape=jax.ShapeDtypeStruct((COLS * CH, NY), f32),
        in_specs=[pl.BlockSpec(memory_space=pltpu.SMEM), vmem, vmem, vmem, vmem],
        out_specs=vmem,
        scratch_shapes=[
            pltpu.VMEM((512, P_SIZE), bf16),
            pltpu.VMEM((CH, P_SIZE), f32),
            pltpu.VMEM((256, F), f32),
            pltpu.VMEM((4, 40, 256), i32),
            pltpu.VMEM((4, 40, 256), i32),
            pltpu.VMEM((3, 136, 256), i32),
            pltpu.VMEM((2, 3, 136, 256), i32),
            pltpu.VMEM((NT, NT), bf16),
            pltpu.VMEM((NT, 2 * F), bf16),
            pltpu.VMEM((2, 3, 136, 256), i32),
            pltpu.VMEM((2, 3, 136, 256), i32),
            pltpu.VMEM((COLS + 256, 768), bf16),
            pltpu.VMEM((768, F), bf16),
            pltpu.VMEM((COLS + 256, F), f32),
            pltpu.VMEM((256, F), f32),
            pltpu.VMEM((2, 168, 256), i32),
            pltpu.VMEM((2, 168, 256), i32),
            pltpu.VMEM((2, 136, 256), i32),
            pltpu.VMEM((2, 136, 256), i32),
            pltpu.VMEM((2, 2, 24, 256), i32),
            pltpu.VMEM((2, 640, NY), f32),
            pltpu.VMEM((CX * (CZ + 2 * REACH) * CH, NY), f32),
            dma((4,)), dma((4,)),
            dma((2, 3)), dma((2, 3)),
            dma((2, 3)), dma((2, 3)),
            dma((2,)), dma((2,)),
            dma((2,)), dma((2,)),
            dma((2, 2)), dma((2, 2)),
        ],
        compiler_params=pltpu.CompilerParams(
            collective_id=0, has_side_effects=True, vmem_limit_bytes=48 * 1024 * 1024
        ),
        cost_estimate=pl.CostEstimate(
            flops=8_000_000_000, bytes_accessed=3_000_000, transcendentals=0
        ),
        name="deposit_and_filter",
    )(
        migration_counts.reshape(1, 5),
        particle_drag.reshape(CH, P_SIZE),
        particle_weights.reshape(P_SIZE, NY),
        tile_owner.reshape(1, NT),
        tile_column.reshape(1, NT),
    )
    return out.reshape(CX, CZ, CH, NY)


def solution(mesh):
    in_specs = (
        P("gx", "gz", None, None),
        P("gx", "gz", None, None),
        P("gx", "gz", None),
        P("gx", "gz", None, None),
        P("gx", "gz", None),
    )
    out_specs = P("gx", "gz", None, None)
    return jax.shard_map(local, mesh=mesh, in_specs=in_specs, out_specs=out_specs, check_vma=False)
```

time: 192 us -> 60.6 us (0.32)
  the two profiles are of different devices: /device:TPU:30 before, /device:TPU:8 now
where the time goes in v1:
time: 60.6 us; the launch traced here: 60.4 us
  Pallas kernels  55.2 us (91%)
  local copies, waits for them, and re-layouts  5.09 us (8%)
    pallas_call x1, Pallas kernels, local(): pl.pallas_call(kernel, out_shape=jax.ShapeDtypeStruct((COLS * CH, NY), f3...  55.2 us
    unnamed x11, local copies, waits for them, and re-layouts  5.09 us

profile of v1, /device:TPU:8, one launch (start us, length us, event | category | flops | bytes accessed | tf_op | source)
XLA Modules:
  0.0 60.4 jit_solution(10302751624501008625)
XLA Ops:
  0.0 0.0 copy-start
  0.0 1.0 %copy-done = bf16[1,1,2048,128]{3,2,1,0:T(8,128)(2,1)S(1)} copy-done((bf16[1,1,2048,128]{3,2,1,0:T(8,128)(2,1)S(1)}, bf16[1,1,2048,128]{3,2,1,0:T(8,128)(2,1)}, u32[]{:S(2)}) %copy-start) | copy-done | bytes 524312
  1.0 0.0 copy-start.1
  1.0 0.7 %copy-done.1 = bf16[1,1,4,2048]{3,2,1,0:T(4,128)(2,1)S(1)} copy-done((bf16[1,1,4,2048]{3,2,1,0:T(4,128)(2,1)S(1)}, bf16[1,1,4,2048]{3,2,1,0:T(4,128)(2,1)}, u32[]{:S(2)}) %copy-start.1) | copy-done | bytes 16408
  1.8 0.0 copy-start.2
  1.8 0.7 %copy-done.2 = s32[1,1,384,1]{2,3,1,0:T(1,128)S(1)} copy-done((s32[1,1,384,1]{2,3,1,0:T(1,128)S(1)}, s32[1,1,384,1]{2,3,1,0:T(1,128)}, u32[]{:S(2)}) %copy-start.2) | copy-done | bytes 1560
  2.4 0.0 copy-start.3
  2.4 0.7 %copy-done.3 = s32[1,1,384]{2,1,0:T(1,128)S(1)} copy-done((s32[1,1,384]{2,1,0:T(1,128)S(1)}, s32[1,1,384]{2,1,0:T(1,128)}, u32[]{:S(2)}) %copy-start.3) | copy-done | bytes 1560
  3.1 0.0 copy-start.4
  3.1 0.7 %copy-done.4 = s32[1,1,5]{2,1,0:T(1,128)S(1)} copy-done((s32[1,1,5]{2,1,0:T(1,128)S(1)}, s32[1,1,5]{2,1,0:T(1,128)}, u32[]{:S(2)}) %copy-start.4) | copy-done | bytes 44
  3.8 55.2 %deposit_and_filter.1 = f32[4096,128]{1,0:T(8,128)S(1)} custom-call(s32[1,5]{1,0:T(1,128)S(1)} %bitcast.11, bf16[4,2048]{1,0:T(4,128)(2,1)S(1)} %bitcast.8, bf16[2048,128]{1,0:T(8,128)(2,1)S(1)} %bitcast.7, s32[1,384]{1,0:T(1,128)S(1)} %bitcast.9, s32[1,384]{1,0:T(1,128)S(1)} %bitcast.10), custom_call_target="tpu_custom_call" | custom-call | flops 8000000000 | bytes 3000000 | tf_op jit(solution)/shard_map/deposit_and_filter/pallas_call | solution.py:377
  59.0 1.3 %copy.7 = f32[32,32,4,128]{3,2,1,0:T(4,128)} copy(f32[32,32,4,128]{3,2,1,0:T(4,128)S(1)} %bitcast.6) | data formatting | bytes 4194304
Async XLA Ops:
  0.0 1.0 %copy-start = (bf16[1,1,2048,128]{3,2,1,0:T(8,128)(2,1)S(1)}, bf16[1,1,2048,128]{3,2,1,0:T(8,128)(2,1)}, u32[]{:S(2)}) copy-start(bf16[1,1,2048,128]{3,2,1,0:T(8,128)(2,1)} %param.6) | copy-start | bytes 1572868
  1.0 0.7 %copy-start.1 = (bf16[1,1,4,2048]{3,2,1,0:T(4,128)(2,1)S(1)}, bf16[1,1,4,2048]{3,2,1,0:T(4,128)(2,1)}, u32[]{:S(2)}) copy-start(bf16[1,1,4,2048]{3,2,1,0:T(4,128)(2,1)} %param.5) | copy-start | bytes 49156
  1.8 0.7 %copy-start.2 = (s32[1,1,384,1]{2,3,1,0:T(1,128)S(1)}, s32[1,1,384,1]{2,3,1,0:T(1,128)}, u32[]{:S(2)}) copy-start(s32[1,1,384,1]{2,3,1,0:T(1,128)} %param.8) | copy-start | bytes 4612
  2.4 0.7 %copy-start.3 = (s32[1,1,384]{2,1,0:T(1,128)S(1)}, s32[1,1,384]{2,1,0:T(1,128)}, u32[]{:S(2)}) copy-start(s32[1,1,384]{2,1,0:T(1,128)} %param.9) | copy-start | bytes 4612
  3.1 0.7 %copy-start.4 = (s32[1,1,5]{2,1,0:T(1,128)S(1)}, s32[1,1,5]{2,1,0:T(1,128)}, u32[]{:S(2)}) copy-start(s32[1,1,5]{2,1,0:T(1,128)} %param.7) | copy-start | bytes 64

commit v2 on v1

v2 whole, which is shorter than its diff:
```python
import math

import jax
import jax.numpy as jnp
from jax import lax
from jax.experimental import pallas as pl
from jax.experimental.pallas import tpu as pltpu
from jax.sharding import PartitionSpec as P

CX = 32
CZ = 32
NY = 128
CH = 4
P_SIZE = 2048
G = 8
REACH = 4
M = 256
KT = 128
NT = 384
F = CH * NY
MOVED_AT = P_SIZE - 4 * M
KEPT = (P_SIZE - M) // G
CHUNKS = ((0, 136), (136, 104), (240, 64), (304, 72))
MOVED_ROW = 240
UNPACKED = (0, 128, 256, 320)
LIST = 376
COLS = CX * CZ
MESH = pl.DeviceIdType.MESH
f32, bf16, i32 = jnp.float32, jnp.bfloat16, jnp.int32
HIGHEST = lax.Precision.HIGHEST


def gauss_taps():
    raw_values = [math.exp(-k * k / 8.0) for k in range(-REACH, REACH + 1)]
    total = sum(raw_values)
    return [v / total for v in raw_values]


TAPS = gauss_taps()


def iota(shape, dim):
    return lax.broadcasted_iota(i32, shape, dim)


def eye():
    return iota((128, 128), 0) == iota((128, 128), 1)


def to_row(column):
    rows = []
    for i in range(0, column.shape[0], 128):
        part = column[i : i + 128]
        shape = (part.shape[0], 128)
        rows.append(
            jnp.sum(jnp.where(iota(shape, 0) == iota(shape, 1), part, 0.0), axis=0, keepdims=True)
        )
    return rows


def to_column(row):
    return jnp.sum(jnp.where(eye(), row, 0.0), axis=1, keepdims=True)


def coded(rows):
    top = jnp.maximum(jnp.max(jnp.abs(rows), axis=1, keepdims=True), 1e-30)
    exponent = jnp.ceil(jnp.log2(top)) - 15.0
    q = jnp.floor(rows * jnp.exp2(-exponent) + 0.5)
    q = jnp.clip(q, -32767.0, 32767.0).astype(i32)
    return (q[:, : F // 2] << 16) | (q[:, F // 2 :] & 0xFFFF), exponent


def integers(packed):
    return jnp.concatenate([packed >> 16, (packed << 16) >> 16], axis=1)


def halves(packed):
    q = integers(packed)
    return (q >> 8).astype(f32).astype(bf16), (q & 255).astype(f32).astype(bf16)


def info_rows(*rows):
    row_id = iota((8, 128), 0)
    block = jnp.zeros((8, 128), i32)
    for i, row in enumerate(rows):
        block = jnp.where(row_id == i, row.astype(i32), block)
    return jnp.concatenate([block, jnp.zeros((8, 128), i32)], axis=1)


def kernel(
    cnt_hbm, drag_hbm, w_hbm, own_hbm, col_hbm, out_ref,
    cnt, drag_ref, w_ref, own_ref, col_ref,
    lhs, dragk, tf, mo, mr, ls, lr, plc, u, xs, xr, rhs, sx, edge, hx, hxr, hz, hzr, ho, hor, hc, hcr, part_x, zx, ax,
    in_s, m_s, m_r, t_s, t_r, x_s, x_r, hx_s, hx_r, hz_s, hz_r, ho_s, ho_r, hc_s, hc_r,
):
    na, nb = lax.axis_size("gx"), lax.axis_size("gz")
    a, b = lax.axis_index("gx"), lax.axis_index("gz")
    a_up, a_dn = lax.rem(a + 1, na), lax.rem(a + na - 1, na)
    b_up, b_dn = lax.rem(b + 1, nb), lax.rem(b + nb - 1, nb)
    odd = lax.rem(b, 2)
    flip = b + 1 - 2 * odd
    b_up2, b_dn2 = lax.rem(b + 2, nb), lax.rem(b + nb - 2, nb)
    relay = jnp.where(odd == 0, b_up2, b_dn2)
    sides_x = ((a_up, b), (a_dn, b))
    sides_z = ((a, b_up), (a, b_dn))
    barrier = pltpu.get_barrier_semaphore()
    for other in sides_x + sides_z + ((a, b_up2), (a, b_dn2)):
        pl.semaphore_signal(barrier, inc=1, device_id=other, device_id_type=MESH)
    fetches = []
    for i, (src, dst) in enumerate(
        ((cnt_hbm, cnt), (drag_hbm, drag_ref), (w_hbm, w_ref), (own_hbm, own_ref), (col_hbm, col_ref))
    ):
        fetch = pltpu.make_async_copy(src, dst, in_s.at[i])
        fetch.start()
        fetches.append(fetch)

    def send(src, dst, s_sem, r_sem, to):
        copy = pltpu.make_async_remote_copy(
            src_ref=src, dst_ref=dst, send_sem=s_sem, recv_sem=r_sem,
            device_id=to, device_id_type=MESH,
        )
        copy.start()
        return copy

    gap = iota((NY, NY), 0) - iota((NY, NY), 1)
    band = jnp.zeros((NY, NY), f32)
    for k in range(2 * REACH + 1):
        band = jnp.where(gap == k - REACH, TAPS[k], band)

    def along_y(rows):
        return jnp.dot(rows, band, precision=HIGHEST, preferred_element_type=f32)

    for fetch in fetches[:2]:
        fetch.wait()
    slot = iota((1, P_SIZE), 1)
    drag = drag_ref[...].astype(f32)
    late, late_drag = slot[:, MOVED_AT:], drag[:, MOVED_AT:]
    t_id = iota((32, P_SIZE - MOVED_AT), 0)
    start = cnt[0, 0]
    for d in range(4):
        rel = late - start
        group = jnp.where((rel >= 0) & (rel < cnt[0, d + 1]), rel >> 3, -1)
        start = start + cnt[0, d + 1]
        mask = group == t_id
        for c in range(CH):
            lhs[d * 128 + c * 32 : d * 128 + c * 32 + 32, :] = jnp.where(
                mask, late_drag[c : c + 1, :], 0.0
            ).astype(bf16)
    fetches[2].wait()
    moved = along_y(
        jnp.dot(lhs[...], w_ref[MOVED_AT:P_SIZE, :], preferred_element_type=f32)
    )
    for d in range(4):
        for c in range(CH):
            tf[d * 32 : d * 32 + 32, c * NY : (c + 1) * NY] = moved[
                d * 128 + c * 32 : d * 128 + c * 32 + 32, :
            ]
    v, e = coded(tf[0:128, :])
    info = info_rows(to_row(e)[0])
    for d in range(4):
        mo[d, 0:32, :] = v[d * 32 : d * 32 + 32, :]
        mo[d, 32:40, :] = info
    dragk[...] = jnp.where(slot < cnt[0, 0], drag, 0.0)
    near = (iota((32, 256), 1) >> 3) == iota((32, 256), 0)
    copies, list_copies, m_copies = [], [], {}

    def ship(i):
        at, size = CHUNKS[i]
        copy = send(
            ls.at[pl.ds(at, size)], lr.at[0, pl.ds(at, size)], t_s.at[0, i], t_r.at[0, i], (a, flip)
        )
        copies.append(copy)
        list_copies.append(copy)

    for fetch in fetches[3:]:
        fetch.wait()
    own_codes, own_cols = own_ref[...], col_ref[...]
    for half, groups in ((0, range(0, 4)), (1, range(4, 7))):
        for g in groups:
            part = dragk[:, g * 256 : (g + 1) * 256]
            rows = jnp.concatenate(
                [jnp.where(near, part[c : c + 1, :], 0.0) for c in range(CH)], axis=0
            )
            made = along_y(
                jnp.dot(
                    rows.astype(bf16), w_ref[g * 256 : (g + 1) * 256, :], preferred_element_type=f32
                )
            )
            for c in range(CH):
                tf[g * 32 : g * 32 + 32, c * NY : (c + 1) * NY] = made[c * 32 : c * 32 + 32, :]
        if half:
            tf[KEPT:256, :] = jnp.zeros((256 - KEPT, F), f32)
        v, e = coded(tf[half * 128 : half * 128 + 128, :])
        at, size = CHUNKS[half]
        ls[at : at + size - 8, :] = v[0 : size - 8, :]
        if half:
            info = info_rows(to_row(e)[0])
        else:
            info = info_rows(
                to_row(e)[0], *(r[:, i : i + 128] for r in (own_codes, own_cols) for i in (0, 128, 256))
            )
        ls[at + size - 8 : at + size, :] = info
        if not half:
            pl.semaphore_wait(barrier, 6)
        ship(half)
        if not half:
            for d, to in ((2, sides_z[0]), (3, sides_z[1]), (0, sides_x[0]), (1, sides_x[1])):
                m_copies[d] = send(mo.at[d], mr.at[d], m_s.at[d], m_r.at[d], to)
                copies.append(m_copies[d])

    lane = iota((1, 128), 1)
    e_row = jnp.zeros((1, 128), i32)
    for d in (0, 1, 2, 3):
        m_copies[d].wait_recv()
        at = MOVED_ROW + d * 32
        ls[at : at + 32, :] = mr[d, 0:32, :]
        e_row = jnp.where((lane >> 5) == d, mr[d, 32:33, 0:128], e_row)
        if d == 1:
            ship(2)
    ls[MOVED_ROW + 128 : MOVED_ROW + 136, :] = info_rows(e_row)
    ship(3)

    before = (iota((NT, NT), 0) < iota((NT, NT), 1)).astype(f32).astype(bf16)
    slot_id = iota((KT, NT), 0).astype(f32)
    sub3 = iota((8, NT), 0)
    lane3 = iota((8, NT), 1)
    u[:, KEPT:256, :] = jnp.zeros((3, 256 - KEPT, 2 * F), bf16)

    def unpack(j, part, i):
        at, size = CHUNKS[i]
        rows = size if i == 2 else size - 8
        hi, lo = halves(part[at : at + rows, :])
        to = UNPACKED[i]
        u[j, to : to + rows, 0:F] = hi
        u[j, to : to + rows, F : 2 * F] = lo

    def placing(j, part, step_z):
        info = part[128:136, 0:128]
        codes = jnp.concatenate([info[1:2], info[2:3], info[3:4]], axis=1)
        live = (sub3 < 3) & ((lane3 < KEPT) | (lane3 >= 256))
        hit = (codes == 3 * sub3 + 1 + step_z) & live
        ranks = jnp.dot(hit.astype(f32).astype(bf16), before, preferred_element_type=f32)
        pos = jnp.where(hit, ranks, -1.0)
        for s in range(3):
            plc[j, s * KT : (s + 1) * KT, :] = (
                (pos[s : s + 1, :] == slot_id).astype(f32).astype(bf16)
            )

    x_copies = {}

    def compact(j, part):
        infos = [part[at + size - 8 : at + size, 0:128] for at, size in CHUNKS]
        cols = jnp.concatenate([infos[0][4:5], infos[0][5:6], infos[0][6:7]], axis=1)
        exps = jnp.concatenate([infos[0][0:1], infos[1][0:1], infos[3][0:1]], axis=1)
        fields = jnp.zeros((8, NT), f32)
        for i, row in enumerate((cols >> 5, cols & 31, exps, jnp.ones((1, NT), i32))):
            fields = jnp.where(sub3 == i, row.astype(f32), fields)
        got = lax.dot_general(
            fields.astype(bf16), plc[j], (((1,), (1,)), ((), ())), preferred_element_type=f32
        )
        col_f = got[0:1] * 32.0 + got[1:2] - jnp.where(got[3:4] > 0.5, 0.0, 1.0)
        exp_f = got[2:3]
        for n, s in ((0, 2), (1, 0)):
            out = jnp.dot(
                plc[j, s * KT : (s + 1) * KT, :], u[j], preferred_element_type=f32
            ).astype(i32)
            q = (out[:, 0:F] << 8) + out[:, F : 2 * F]
            xs[n, j, 0:128, :] = (q[:, : F // 2] << 16) | (q[:, F // 2 :] & 0xFFFF)
            xs[n, j, 128:136, :] = info_rows(
                col_f[:, s * KT : (s + 1) * KT], exp_f[:, s * KT : (s + 1) * KT]
            )
            x_copies[n, j] = send(
                xs.at[n, j], xr.at[n, j], x_s.at[n, j], x_r.at[n, j], sides_x[n]
            )
            copies.append(x_copies[n, j])
        mid = jnp.dot(plc[j, KT : 2 * KT, :], u[j], preferred_element_type=f32).astype(bf16)
        rhs[j, 0:128, :] = mid[:, 0:F]
        rhs[j, 128:256, :] = mid[:, F : 2 * F]
        return col_f[:, KT : 2 * KT], jnp.exp2(exp_f[:, KT : 2 * KT])

    def one_hot(i, spots):
        row_id = iota((256, 128), 0)
        if i < 4:
            row_col = row_id + 256 * i
        else:
            row_col = ((row_id & 127) >> 2) * CZ + (row_id & 3)
            row_col = row_col + jnp.where(row_id >= 128, CZ - REACH, 0)
        row_col = row_col.astype(f32)
        parts = []
        for col_f, scale in spots:
            h = jnp.where(row_col == col_f, scale, 0.0)
            parts += [(h * 256.0).astype(bf16), h.astype(bf16)]
        return jnp.concatenate(parts, axis=1)

    def arrived(j, spot):
        spots = [spot]
        for n in range(2):
            x_copies[n, j].wait_recv()
            at = 256 * (n + 1)
            hi, lo = halves(xr[n, j, 0:128, :])
            rhs[j, at : at + 128, :] = hi
            rhs[j, at + 128 : at + 256, :] = lo
            got = xr[n, j, 128:136, 0:128].astype(f32)
            spots.append((got[0:1], jnp.exp2(got[1:2])))
        return spots

    def deposit(j, i, spots):
        part = jnp.dot(one_hot(i, spots), rhs[j], preferred_element_type=f32)
        if i < 4:
            at = 128 + i * 256
            if j:
                part = part + sx[at : at + 256, :]
            sx[at : at + 256, :] = part
        else:
            if j:
                part = part + edge[...]
            edge[...] = part

    toward = jnp.where(odd == 0, -1, 1)
    placing(0, ls, 0)
    for i in range(4):
        unpack(0, ls, i)
    relay_copies = []

    def pass_on(i):
        at, size = CHUNKS[i]
        list_copies[i].wait_recv()
        copy = send(
            lr.at[0, pl.ds(at, size)], lr.at[1, pl.ds(at, size)], t_s.at[1, i], t_r.at[1, i], (a, relay)
        )
        copies.append(copy)
        relay_copies.append(copy)

    pass_on(0)
    spot = compact(0, ls)
    placing(1, lr.at[0], toward)
    unpack(1, lr.at[0], 0)
    for i in range(1, 4):
        pass_on(i)
        unpack(1, lr.at[0], i)
    next_spot = compact(1, lr.at[0])
    spots = arrived(0, spot)
    for i in range(5):
        deposit(0, i, spots)
    relay_copies[0].wait_recv()
    placing(2, lr.at[1], -toward)
    unpack(2, lr.at[1], 0)
    for i in range(1, 4):
        relay_copies[i].wait_recv()
        unpack(2, lr.at[1], i)
    last_spot = compact(2, lr.at[1])
    spots = arrived(1, next_spot)
    for i in range(5):
        deposit(1, i, spots)
    spots = arrived(2, last_spot)

    deposit(2, 4, spots)
    z_copies, h_copies, c_copies, o_copies = [], [], [], []
    vc, ec = coded(
        jnp.concatenate(
            [edge[at : at + 16, :] for at in (112, 128 + 112, 0, 128)], axis=0
        )
    )
    info = info_rows(to_row(ec)[0])
    for n in range(2):
        hc[n, 0:32, :] = vc[n * 32 : n * 32 + 32, :]
        hc[n, 32:40, :] = info
        c_copies.append(send(hc.at[n], hcr.at[n], hc_s.at[n], hc_r.at[n], sides_x[n]))

    def banded(shape, out_pos, in_pos):
        apart = in_pos - out_pos
        matrix = jnp.zeros(shape, f32)
        for k in range(2 * REACH + 1):
            matrix = jnp.where(apart == 4 * (k - REACH), TAPS[k], matrix)
        return matrix

    own_x = banded((128, 128), iota((128, 128), 0), iota((128, 128), 1))
    for n, s in ((0, 1), (1, 0)):
        made = jnp.dot(
            own_x, edge[s * 128 : (s + 1) * 128, :], precision=HIGHEST, preferred_element_type=f32
        )
        part_x[s, 0:16, :] = made[0:16, :]
        part_x[s, 16:32, :] = made[112:128, :]
        ve, ee = coded(made[16:112, :])
        hz[n, 0:96, :] = ve
        hz[n, 96:104, :] = info_rows(to_row(ee)[0])
        z_copies.append(send(hz.at[n], hzr.at[n], hz_s.at[n], hz_r.at[n], sides_z[n]))
    for n, i in ((0, 3), (1, 0)):
        deposit(2, i, spots)
        at = COLS if n == 0 else 128
        vx, ex = coded(sx[at : at + 128, :])
        hx[n, 0:128, :] = vx
        hx[n, 128:136, :] = info_rows(to_row(ex)[0])
        h_copies.append(send(hx.at[n], hxr.at[n], hx_s.at[n], hx_r.at[n], sides_x[n]))
    i_out, i_in = iota((32, 32), 0), iota((32, 32), 1)
    far_x = banded(
        (32, 32), jnp.where(i_out < 16, i_out, i_out + 96), jnp.where(i_in < 16, i_in - 16, i_in + 112)
    )
    beyond = []
    for n in range(2):
        c_copies[n].wait_recv()
        scale = jnp.exp2(to_column(hcr[n, 32:33, 0:128].astype(f32)))
        beyond.append(integers(hcr[n, 0:32, :]).astype(f32) * scale[n * 32 : n * 32 + 32])
    outer = []
    for s in range(2):
        rows = jnp.concatenate([v[s * 16 : s * 16 + 16] for v in beyond], axis=0)
        outer.append(
            part_x[s] + jnp.dot(far_x, rows, precision=HIGHEST, preferred_element_type=f32)
        )
    vo, eo = coded(jnp.concatenate(outer, axis=0))
    info = info_rows(to_row(eo)[0])
    for n, s in ((0, 1), (1, 0)):
        ho[n, 0:32, :] = vo[s * 32 : s * 32 + 32, :]
        ho[n, 32:40, :] = info
        o_copies.append(send(ho.at[n], hor.at[n], ho_s.at[n], ho_r.at[n], sides_z[n]))
    copies += z_copies + h_copies + c_copies + o_copies
    deposit(2, 1, spots)
    deposit(2, 2, spots)
    for n in range(2):
        h_copies[n].wait_recv()
    for n in range(2):
        got = hxr[n, 0:128, :]
        scale = jnp.exp2(to_column(hxr[n, 128:129, 0:128].astype(f32)))
        at = 0 if n == 0 else COLS + 128
        sx[at : at + 128, :] = integers(got).astype(f32) * scale

    def taps(term):
        total = term(REACH) * TAPS[REACH]
        for k in range(1, REACH + 1):
            total = total + (term(REACH - k) + term(REACH + k)) * TAPS[REACH + k]
        return total

    EXT = (CZ + 2 * REACH) * CH

    def x_pass(x, _):
        total = taps(lambda k: sx[pl.ds(pl.multiple_of((x + k) * CZ, CZ), CZ), :])
        for c in range(CH):
            ax[pl.ds(x * EXT + 4 * CH + c, CZ, stride=CH), :] = total[:, c * NY : (c + 1) * NY]
        inner = taps(lambda k: ax[pl.ds(x * EXT + 4 * CH + CH * k, (CZ - 8) * CH), :])
        at = pl.multiple_of(x * CZ * CH + 4 * CH, 16)
        out_ref[pl.ds(at, (CZ - 8) * CH), :] = inner
        return 0

    lax.fori_loop(0, CX, x_pass, 0)

    for n in range(2):
        z_copies[n].wait_recv()
        scale = jnp.exp2(to_column(hzr[n, 96:97, 0:128].astype(f32)))
        rows = integers(hzr[n, 0:96, :]).astype(f32) * scale[0:96]
        for c in range(CH):
            zx[n, pl.ds(16 * CH + c, 96, stride=CH), :] = rows[:, c * NY : (c + 1) * NY]
    for n in range(2):
        o_copies[n].wait_recv()
        scale = jnp.exp2(to_column(hor[n, 32:33, 0:128].astype(f32)))
        s = 1 - n
        rows = integers(hor[n, 0:32, :]).astype(f32) * scale[s * 32 : s * 32 + 32]
        for half in range(2):
            for c in range(CH):
                zx[n, pl.ds(half * 112 * CH + c, 16, stride=CH), :] = rows[
                    half * 16 : half * 16 + 16, c * NY : (c + 1) * NY
                ]

    W = 4 * CH

    def z_pass(step, _):
        for part in range(4):
            x = step * 4 + part
            for n in range(2):
                at = x * EXT + (0 if n == 0 else (CZ + REACH) * CH)
                ax[pl.ds(pl.multiple_of(at, 8), W), :] = zx[n, pl.ds(pl.multiple_of(x * W, W), W), :]
        for part in range(4):
            x = step * 4 + part
            for z in (0, CZ - REACH):
                total = taps(lambda k: ax[pl.ds(x * EXT + CH * (z + k), W), :])
                out_ref[pl.ds(pl.multiple_of(x * CZ * CH + z * CH, W), W), :] = total
        return 0

    lax.fori_loop(0, CX // 4, z_pass, 0)
    for copy in copies:
        copy.wait_send()


def local(particle_drag, particle_weights, migration_counts, tile_owner, tile_column):
    vmem = pl.BlockSpec(memory_space=pltpu.VMEM)
    dma = pltpu.SemaphoreType.DMA
    hbm = pl.BlockSpec(memory_space=pltpu.HBM)
    out = pl.pallas_call(
        kernel,
        out_shape=jax.ShapeDtypeStruct((COLS * CH, NY), f32),
        in_specs=[hbm] * 5,
        out_specs=vmem,
        scratch_shapes=[
            pltpu.SMEM((1, 5), i32),
            pltpu.VMEM((CH, P_SIZE), bf16),
            pltpu.VMEM((P_SIZE, NY), bf16),
            pltpu.VMEM((1, NT), i32),
            pltpu.VMEM((1, NT), i32),
            pltpu.VMEM((512, P_SIZE - MOVED_AT), bf16),
            pltpu.VMEM((CH, P_SIZE), f32),
            pltpu.VMEM((256, F), f32),
            pltpu.VMEM((4, 40, 256), i32),
            pltpu.VMEM((4, 40, 256), i32),
            pltpu.VMEM((LIST, 256), i32),
            pltpu.VMEM((2, LIST, 256), i32),
            pltpu.VMEM((3, NT, NT), bf16),
            pltpu.VMEM((3, NT, 2 * F), bf16),
            pltpu.VMEM((2, 3, 136, 256), i32),
            pltpu.VMEM((2, 3, 136, 256), i32),
            pltpu.VMEM((3, 768, F), bf16),
            pltpu.VMEM((COLS + 256, F), f32),
            pltpu.VMEM((256, F), f32),
            pltpu.VMEM((2, 136, 256), i32),
            pltpu.VMEM((2, 136, 256), i32),
            pltpu.VMEM((2, 104, 256), i32),
            pltpu.VMEM((2, 104, 256), i32),
            pltpu.VMEM((2, 40, 256), i32),
            pltpu.VMEM((2, 40, 256), i32),
            pltpu.VMEM((2, 40, 256), i32),
            pltpu.VMEM((2, 40, 256), i32),
            pltpu.VMEM((2, 32, F), f32),
            pltpu.VMEM((2, 512, NY), f32),
            pltpu.VMEM((CX * (CZ + 2 * REACH) * CH, NY), f32),
            dma((5,)),
            dma((4,)), dma((4,)),
            dma((2, 4)), dma((2, 4)),
            dma((2, 3)), dma((2, 3)),
            dma((2,)), dma((2,)),
            dma((2,)), dma((2,)),
            dma((2,)), dma((2,)),
            dma((2,)), dma((2,)),
        ],
        compiler_params=pltpu.CompilerParams(
            collective_id=0, has_side_effects=True, vmem_limit_bytes=48 * 1024 * 1024
        ),
        cost_estimate=pl.CostEstimate(
            flops=8_000_000_000, bytes_accessed=3_000_000, transcendentals=0
        ),
        name="deposit_and_filter",
    )(
        migration_counts.reshape(1, 5),
        particle_drag.reshape(CH, P_SIZE),
        particle_weights.reshape(P_SIZE, NY),
        tile_owner.reshape(1, NT),
        tile_column.reshape(1, NT),
    )
    return out.reshape(CX, CZ, CH, NY)


def solution(mesh):
    in_specs = (
        P("gx", "gz", None, None),
        P("gx", "gz", None, None),
        P("gx", "gz", None),
        P("gx", "gz", None, None),
        P("gx", "gz", None),
    )
    out_specs = P("gx", "gz", None, None)
    return jax.shard_map(local, mesh=mesh, in_specs=in_specs, out_specs=out_specs, check_vma=False)
```

time: 60.6 us -> 50.8 us (0.84)
  the two profiles are of different devices: /device:TPU:8 before, /device:TPU:2 now
where the time goes in v2:
time: 50.8 us; the launch traced here: 50.5 us
  Pallas kernels  45.4 us (89%)
  local copies, waits for them, and re-layouts  5.09 us (10%)
    pallas_call x1, Pallas kernels, local(): pl.pallas_call(kernel, out_shape=jax.ShapeDtypeStruct((COLS * CH, NY), f3...  45.4 us
    unnamed x11, local copies, waits for them, and re-layouts  5.09 us

profile of v2, /device:TPU:2, one launch (start us, length us, event | category | flops | bytes accessed | tf_op | source)
XLA Modules:
  0.0 50.5 jit_solution(7107105162939545244)
XLA Ops:
  0.0 0.0 copy-start
  0.0 1.0 %copy-done = bf16[1,1,2048,128]{3,2,1,0:T(8,128)(2,1)S(1)} copy-done((bf16[1,1,2048,128]{3,2,1,0:T(8,128)(2,1)S(1)}, bf16[1,1,2048,128]{3,2,1,0:T(8,128)(2,1)}, u32[]{:S(2)}) %copy-start) | copy-done | bytes 524312
  1.0 0.0 copy-start.1
  1.0 0.7 %copy-done.1 = bf16[1,1,4,2048]{3,2,1,0:T(4,128)(2,1)S(1)} copy-done((bf16[1,1,4,2048]{3,2,1,0:T(4,128)(2,1)S(1)}, bf16[1,1,4,2048]{3,2,1,0:T(4,128)(2,1)}, u32[]{:S(2)}) %copy-start.1) | copy-done | bytes 16408
  1.8 0.0 copy-start.2
  1.8 0.7 %copy-done.2 = s32[1,1,384,1]{2,3,1,0:T(1,128)S(1)} copy-done((s32[1,1,384,1]{2,3,1,0:T(1,128)S(1)}, s32[1,1,384,1]{2,3,1,0:T(1,128)}, u32[]{:S(2)}) %copy-start.2) | copy-done | bytes 1560
  2.4 0.0 copy-start.3
  2.4 0.7 %copy-done.3 = s32[1,1,384]{2,1,0:T(1,128)S(1)} copy-done((s32[1,1,384]{2,1,0:T(1,128)S(1)}, s32[1,1,384]{2,1,0:T(1,128)}, u32[]{:S(2)}) %copy-start.3) | copy-done | bytes 1560
  3.1 0.0 copy-start.4
  3.1 0.7 %copy-done.4 = s32[1,1,5]{2,1,0:T(1,128)S(1)} copy-done((s32[1,1,5]{2,1,0:T(1,128)S(1)}, s32[1,1,5]{2,1,0:T(1,128)}, u32[]{:S(2)}) %copy-start.4) | copy-done | bytes 44
  3.8 45.4 %deposit_and_filter.1 = f32[4096,128]{1,0:T(8,128)S(1)} custom-call(s32[1,5]{1,0:T(1,128)S(1)} %bitcast.11, bf16[4,2048]{1,0:T(4,128)(2,1)S(1)} %bitcast.8, bf16[2048,128]{1,0:T(8,128)(2,1)S(1)} %bitcast.7, s32[1,384]{1,0:T(1,128)S(1)} %bitcast.9, s32[1,384]{1,0:T(1,128)S(1)} %bitcast.10), custom_call_target="tpu_custom_call" | custom-call | flops 8000000000 | bytes 3000000 | tf_op jit(solution)/shard_map/deposit_and_filter/pallas_call | solution.py:487
  49.2 1.3 %copy.7 = f32[32,32,4,128]{3,2,1,0:T(4,128)} copy(f32[32,32,4,128]{3,2,1,0:T(4,128)S(1)} %bitcast.6) | data formatting | bytes 4194304
Async XLA Ops:
  0.0 1.0 %copy-start = (bf16[1,1,2048,128]{3,2,1,0:T(8,128)(2,1)S(1)}, bf16[1,1,2048,128]{3,2,1,0:T(8,128)(2,1)}, u32[]{:S(2)}) copy-start(bf16[1,1,2048,128]{3,2,1,0:T(8,128)(2,1)} %param.6) | copy-start | bytes 1572868
  1.0 0.7 %copy-start.1 = (bf16[1,1,4,2048]{3,2,1,0:T(4,128)(2,1)S(1)}, bf16[1,1,4,2048]{3,2,1,0:T(4,128)(2,1)}, u32[]{:S(2)}) copy-start(bf16[1,1,4,2048]{3,2,1,0:T(4,128)(2,1)} %param.5) | copy-start | bytes 49156
  1.8 0.7 %copy-start.2 = (s32[1,1,384,1]{2,3,1,0:T(1,128)S(1)}, s32[1,1,384,1]{2,3,1,0:T(1,128)}, u32[]{:S(2)}) copy-start(s32[1,1,384,1]{2,3,1,0:T(1,128)} %param.8) | copy-start | bytes 4612
  2.4 0.7 %copy-start.3 = (s32[1,1,384]{2,1,0:T(1,128)S(1)}, s32[1,1,384]{2,1,0:T(1,128)}, u32[]{:S(2)}) copy-start(s32[1,1,384]{2,1,0:T(1,128)} %param.9) | copy-start | bytes 4612
  3.1 0.7 %copy-start.4 = (s32[1,1,5]{2,1,0:T(1,128)S(1)}, s32[1,1,5]{2,1,0:T(1,128)}, u32[]{:S(2)}) copy-start(s32[1,1,5]{2,1,0:T(1,128)} %param.7) | copy-start | bytes 64

commit v3 on v2

--- a/solution.py
+++ b/solution.py
@@ -88,10 +88,10 @@
 
 
 def kernel(
-    cnt_hbm, drag_hbm, w_hbm, own_hbm, col_hbm, out_ref,
+    cnt_hbm, drag_hbm, w_hbm, own_hbm, col_hbm, out_hbm,
     cnt, drag_ref, w_ref, own_ref, col_ref,
-    lhs, dragk, tf, mo, mr, ls, lr, plc, u, xs, xr, rhs, sx, edge, hx, hxr, hz, hzr, ho, hor, hc, hcr, part_x, zx, ax,
-    in_s, m_s, m_r, t_s, t_r, x_s, x_r, hx_s, hx_r, hz_s, hz_r, ho_s, ho_r, hc_s, hc_r,
+    lhs, dragk, tf, mo, mr, ls, lr, plc, u, xs, xr, rhs, sx, edge, hx, hxr, hz, hzr, ho, hor, hc, hcr, part_x, zx, ax, out_ref,
+    in_s, out_s, m_s, m_r, t_s, t_r, x_s, x_r, hx_s, hx_r, hz_s, hz_r, ho_s, ho_r, hc_s, hc_r,
 ):
     na, nb = lax.axis_size("gx"), lax.axis_size("gz")
     a, b = lax.axis_index("gx"), lax.axis_index("gz")
@@ -437,12 +437,19 @@
         for c in range(CH):
             ax[pl.ds(x * EXT + 4 * CH + c, CZ, stride=CH), :] = total[:, c * NY : (c + 1) * NY]
         inner = taps(lambda k: ax[pl.ds(x * EXT + 4 * CH + CH * k, (CZ - 8) * CH), :])
-        at = pl.multiple_of(x * CZ * CH + 4 * CH, 16)
-        out_ref[pl.ds(at, (CZ - 8) * CH), :] = inner
+        out_ref[x, 4 * CH : (CZ - 4) * CH, :] = inner
         return 0
 
     lax.fori_loop(0, CX, x_pass, 0)
 
+    def leave(at, size, sem):
+        copy = pltpu.make_async_copy(
+            out_ref.at[:, pl.ds(at, size)], out_hbm.at[:, pl.ds(at, size)], out_s.at[sem]
+        )
+        copy.start()
+        return copy
+
+    leaving = [leave(4 * CH, (CZ - 8) * CH, 0)]
     for n in range(2):
         z_copies[n].wait_recv()
         scale = jnp.exp2(to_column(hzr[n, 96:97, 0:128].astype(f32)))
@@ -472,23 +479,41 @@
             x = step * 4 + part
             for z in (0, CZ - REACH):
                 total = taps(lambda k: ax[pl.ds(x * EXT + CH * (z + k), W), :])
-                out_ref[pl.ds(pl.multiple_of(x * CZ * CH + z * CH, W), W), :] = total
+                out_ref[x, z * CH : z * CH + W, :] = total
         return 0
 
     lax.fori_loop(0, CX // 4, z_pass, 0)
+    leaving += [leave(0, W, 1), leave((CZ - 4) * CH, W, 2)]
     for copy in copies:
         copy.wait_send()
+    for copy in leaving:
+        copy.wait()
+
+
+def hand_over(src, dst, held, in_s, out_s):
+    part = CX // 8
+    came, went = [], []
+    for i in range(8):
+        rows = pl.ds(i * part, part)
+        came.append(pltpu.make_async_copy(src.at[rows], held.at[rows], in_s.at[i]))
+        came[i].start()
+    for i in range(8):
+        rows = pl.ds(i * part, part)
+        came[i].wait()
+        went.append(pltpu.make_async_copy(held.at[rows], dst.at[rows], out_s.at[i]))
+        went[i].start()
+    for copy in went:
+        copy.wait()
 
 
 def local(particle_drag, particle_weights, migration_counts, tile_owner, tile_column):
-    vmem = pl.BlockSpec(memory_space=pltpu.VMEM)
     dma = pltpu.SemaphoreType.DMA
     hbm = pl.BlockSpec(memory_space=pltpu.HBM)
     out = pl.pallas_call(
         kernel,
-        out_shape=jax.ShapeDtypeStruct((COLS * CH, NY), f32),
+        out_shape=jax.ShapeDtypeStruct((CX, CZ * CH, NY), f32),
         in_specs=[hbm] * 5,
-        out_specs=vmem,
+        out_specs=hbm,
         scratch_shapes=[
             pltpu.SMEM((1, 5), i32),
             pltpu.VMEM((CH, P_SIZE), bf16),
@@ -520,7 +545,8 @@
             pltpu.VMEM((2, 32, F), f32),
             pltpu.VMEM((2, 512, NY), f32),
             pltpu.VMEM((CX * (CZ + 2 * REACH) * CH, NY), f32),
-            dma((5,)),
+            pltpu.VMEM((CX, CZ * CH, NY), f32),
+            dma((5,)), dma((3,)),
             dma((4,)), dma((4,)),
             dma((2, 4)), dma((2, 4)),
             dma((2, 3)), dma((2, 3)),
@@ -530,7 +556,7 @@
             dma((2,)), dma((2,)),
         ],
         compiler_params=pltpu.CompilerParams(
-            collective_id=0, has_side_effects=True, vmem_limit_bytes=48 * 1024 * 1024
+            collective_id=0, has_side_effects=True, vmem_limit_bytes=56500 * 1024
         ),
         cost_estimate=pl.CostEstimate(
             flops=8_000_000_000, bytes_accessed=3_000_000, transcendentals=0
@@ -543,6 +569,15 @@
         tile_owner.reshape(1, NT),
         tile_column.reshape(1, NT),
     )
+    out = pl.pallas_call(
+        hand_over,
+        out_shape=jax.ShapeDtypeStruct(out.shape, f32),
+        in_specs=[hbm],
+        out_specs=hbm,
+        scratch_shapes=[pltpu.VMEM((CX, CZ * CH, NY), f32), dma((8,)), dma((8,))],
+        compiler_params=pltpu.CompilerParams(vmem_limit_bytes=56500 * 1024),
+        name="hand_over",
+    )(out)
     return out.reshape(CX, CZ, CH, NY)
 
 

time: 50.8 us -> 49.3 us (0.970)
  the two profiles are of different devices: /device:TPU:2 before, /device:TPU:30 now
where the time goes in v3:
time: 49.3 us; the launch traced here: 49.2 us
  Pallas kernels  49.1 us (100%)
    pallas_call x1, Pallas kernels, local(): pl.pallas_call(kernel, out_shape=jax.ShapeDtypeStruct((CX, CZ * CH, NY),...  46.8 us
    pallas_call x1, Pallas kernels, local(): pl.pallas_call(hand_over, out_shape=jax.ShapeDtypeStruct(out.shape, f32),...  2.39 us

profile of v3, /device:TPU:30, one launch (start us, length us, event | category | flops | bytes accessed | tf_op | source)
XLA Modules:
  0.0 49.2 jit_solution(73483812958326573)
XLA Ops:
  0.0 46.8 %deposit_and_filter.1.src = f32[32,128,128]{2,1,0:T(8,128)} custom-call(s32[1,5]{1,0:T(1,128)} %bitcast.10, bf16[4,2048]{1,0:T(4,128)(2,1)} %bitcast.7, bf16[2048,128]{1,0:T(8,128)(2,1)} %bitcast.6, s32[1,384]{1,0:T(1,128)} %bitcast.8, s32[1,384]{1,0:T(1,128)} %bitcast.9), custom_call_target="tpu_custom_call" | custom-call | flops 8000000000 | bytes 3000000 | tf_op jit(solution)/shard_map/deposit_and_filter/pallas_call | solution.py:512
  46.8 2.4 %hand_over.1 = f32[32,128,128]{2,1,0:T(8,128)} custom-call(f32[32,128,128]{2,1,0:T(8,128)} %deposit_and_filter.1.src), custom_call_target="tpu_custom_call" | custom-call | tf_op jit(solution)/shard_map/hand_over/pallas_call | solution.py:572
